TPU v7x, 512 devices: a whole 4x4x16 slice. The times are simulated.
512 devices in a mesh: row: 16 (over z_lo, core), col: 32 (over x, y, z_hi).
Axes of the slice: x: 4, y: 4, z: 16 (z_hi: 2, z_lo: 8; z = z_hi * 8 + z_lo), core: 2. Of those that a mesh axis runs over, the one named last changes fastest.
Arguments:
- features: bfloat16 [128, 512, 128], P('row', 'col'), may hold values from -6 to 6
- cotangent: bfloat16 [128, 512, 128], P('row', 'col'), may hold values from -12 to 12
- w_qkv: bfloat16 [128, 384], replicated, may hold values from -0.5 to 0.5
- w_out: bfloat16 [128, 128], replicated, may hold values from -0.5 to 0.5
- cos_scale: float32 [2], replicated, may hold values from 4 to 16
Outputs:
- grad_features: bfloat16 [128, 512, 128], P('row', 'col')
- grad_w_qkv: float32 [128, 384], replicated
- grad_w_out: float32 [128, 128], replicated
- grad_scale: float32 [2], replicated
All inputs are finite; a program needn't handle non-finite values.
Results may differ from a plain program's by a relative error of at most 0.0085.
Values may be sent and summed in bfloat16 or wider, within the bound.
No kernel may reach another device: no remote copies, remote signals or barrier semaphores. Data moves between devices by JAX's collectives and lax.ppermute only.
A program may use at most 128 MiB of HBM per device.

v0:
```python
from functools import reduce

import jax
import jax.numpy as jnp
from jax import lax
from jax.sharding import PartitionSpec as P

HEADS = 2
HEAD_DIM = 64
RADIUS = 3


EPSILON = 1e-06


def extended(cells, sides, width):
    for axis, dim in sides:
        count = lax.axis_size(axis)
        ends = count - 1
        head = lax.slice_in_dim(cells, 0, width, axis=dim)
        tail = lax.slice_in_dim(cells, cells.shape[dim] - width, cells.shape[dim], axis=dim)
        cells = jnp.concatenate(
            [
                lax.ppermute(tail, axis, [(i, (i + 1) % count) for i in range(ends)]),
                cells,
                lax.ppermute(head, axis, [((i + 1) % count, i) for i in range(ends)]),
            ],
            axis=dim,
        )
    return cells


def head_sums(left, right):
    product = (left * right).reshape(left.shape[:2] + (HEADS, HEAD_DIM))
    totals = jnp.sum(product, axis=-1)
    return jnp.stack([totals[:, :, head] for head in range(HEADS)], axis=0)


def spread_heads(scalars):
    shape = scalars.shape[1:] + (HEAD_DIM,)
    return jnp.concatenate(
        [jnp.broadcast_to(scalars[head][..., None], shape) for head in range(HEADS)], axis=-1
    )


def unit_heads(values):
    wide = values.astype(jnp.float32)
    inverse = lax.rsqrt(head_sums(wide, wide) + EPSILON)
    return (wide * spread_heads(inverse), inverse)


def unit_backward(grad_unit, unit, inverse):
    along_unit = head_sums(unit, grad_unit)
    return (grad_unit - unit * spread_heads(along_unit)) * spread_heads(inverse)


def grid_mask(first_row, first_col, count_rows, count_cols, rows_all, cols_all):
    rows_here = first_row + jnp.arange(count_rows, dtype=jnp.int32)
    cols_here = first_col + jnp.arange(count_cols, dtype=jnp.int32)
    row_valid = (rows_here >= 0) & (rows_here < rows_all)
    col_valid = (cols_here >= 0) & (cols_here < cols_all)
    return row_valid[:, None] & col_valid[None, :]


def window_pass(q_unit, k_unit, values, d_attn, inside, cos_scale):
    out_rows = q_unit.shape[0]
    out_cols = q_unit.shape[1]
    model_width = q_unit.shape[2]
    window_span = 2 * RADIUS + 1
    factor = cos_scale[:, None, None]
    places = [
        (shift_row, shift_col)
        for shift_row in range(window_span)
        for shift_col in range(window_span)
    ]
    cosines = []
    expos = []
    for shift_row, shift_col in places:
        key_slice = k_unit[shift_row : shift_row + out_rows, shift_col : shift_col + out_cols]
        cosine = head_sums(q_unit, key_slice)
        live_mask = inside[shift_row : shift_row + out_rows, shift_col : shift_col + out_cols][None]
        cosines.append(cosine)
        expos.append(jnp.where(live_mask, jnp.exp(factor * cosine), 0.0))
    denominator = reduce(jnp.add, expos)
    weights = [expo / denominator for expo in expos]
    mixed_out = jnp.zeros(q_unit.shape, jnp.float32)
    dot_terms = []
    for position, (shift_row, shift_col) in enumerate(places):
        value_slice = values[shift_row : shift_row + out_rows, shift_col : shift_col + out_cols]
        mixed_out = mixed_out + spread_heads(weights[position]) * value_slice
        dot_terms.append(head_sums(d_attn, value_slice))
    center = reduce(
        jnp.add, [weights[position] * dot_terms[position] for position in range(len(places))]
    )
    grad_q = jnp.zeros(q_unit.shape, jnp.float32)
    grad_kv = jnp.zeros(k_unit.shape[:2] + (2 * model_width,), jnp.float32)
    scale_terms = jnp.zeros(cosines[0].shape, jnp.float32)
    for position, (shift_row, shift_col) in enumerate(places):
        key_slice = k_unit[shift_row : shift_row + out_rows, shift_col : shift_col + out_cols]
        grad_score = weights[position] * (dot_terms[position] - center)
        scale_terms = scale_terms + grad_score * cosines[position]
        scaled = spread_heads(factor * grad_score)
        grad_q = grad_q + scaled * key_slice
        kv_term = jnp.concatenate(
            [scaled * q_unit, spread_heads(weights[position]) * d_attn], axis=-1
        )
        grad_kv = grad_kv.at[
            shift_row : shift_row + out_rows, shift_col : shift_col + out_cols
        ].add(kv_term)
    return (mixed_out, grad_q, grad_kv, scale_terms)


def fold_rims(grad_ext, returned, tile_rows, tile_cols):
    margin = RADIUS
    inner = grad_ext[margin : margin + tile_rows, margin : margin + tile_cols]
    far_row = tile_rows + 3 * margin
    far_col = tile_cols + 3 * margin
    mid_rows = slice(2 * margin, 2 * margin + tile_rows)
    mid_cols = slice(2 * margin, 2 * margin + tile_cols)
    inner = inner.at[:margin].add(returned[:margin, mid_cols])
    inner = inner.at[tile_rows - margin :].add(returned[far_row:, mid_cols])
    inner = inner.at[:, :margin].add(returned[mid_rows, :margin])
    inner = inner.at[:, tile_cols - margin :].add(returned[mid_rows, far_col:])
    inner = inner.at[:margin, :margin].add(returned[:margin, :margin])
    inner = inner.at[:margin, tile_cols - margin :].add(returned[:margin, far_col:])
    inner = inner.at[tile_rows - margin :, :margin].add(returned[far_row:, :margin])
    inner = inner.at[tile_rows - margin :, tile_cols - margin :].add(returned[far_row:, far_col:])
    return inner


def on_device(features, cotangent, w_qkv, w_out, cos_scale):
    tile_rows, tile_cols, model_width = features.shape
    margin = RADIUS
    flat_in = features.reshape(-1, model_width)
    flat_grad = cotangent.reshape(-1, model_width)
    projected = jnp.dot(flat_in, w_qkv, preferred_element_type=jnp.float32)
    projected = projected.astype(jnp.bfloat16).reshape(tile_rows, tile_cols, 3 * model_width)
    query_raw = projected[..., :model_width]
    keyval = projected[..., model_width:]
    d_attn = lax.dot_general(
        flat_grad, w_out, (((1,), (1,)), ((), ())), preferred_element_type=jnp.float32
    )
    d_attn = d_attn.astype(jnp.bfloat16).reshape(tile_rows, tile_cols, model_width)
    row_start = lax.axis_index("row") * tile_rows
    col_start = lax.axis_index("col") * tile_cols
    rows_all = lax.axis_size("row") * tile_rows
    cols_all = lax.axis_size("col") * tile_cols
    keyval_ext = extended(keyval, (("row", 0), ("col", 1)), margin)
    inside = grid_mask(
        row_start - margin,
        col_start - margin,
        tile_rows + 2 * margin,
        tile_cols + 2 * margin,
        rows_all,
        cols_all,
    )
    q_unit, q_inverse = unit_heads(query_raw)
    k_unit, k_inverse = unit_heads(keyval_ext[..., :model_width])
    values = keyval_ext[..., model_width:].astype(jnp.float32)
    mixed_out, grad_q, grad_ext, scale_terms = window_pass(
        q_unit, k_unit, values, d_attn.astype(jnp.float32), inside, cos_scale
    )
    returned = extended(grad_ext.astype(jnp.bfloat16), (("row", 0), ("col", 1)), margin).astype(
        grad_ext.dtype
    )
    folded = fold_rims(grad_ext, returned, tile_rows, tile_cols)
    grad_k_own = folded[..., :model_width]
    grad_v_own = folded[..., model_width:]
    k_unit_own = k_unit[margin : margin + tile_rows, margin : margin + tile_cols]
    k_inverse_own = k_inverse[:, margin : margin + tile_rows, margin : margin + tile_cols]
    attn_out = mixed_out.astype(jnp.bfloat16).reshape(-1, model_width)
    out_term = lax.dot_general(
        attn_out, flat_grad, (((0,), (0,)), ((), ())), preferred_element_type=jnp.float32
    )
    grad_query = unit_backward(grad_q, q_unit, q_inverse)
    grad_key = unit_backward(grad_k_own, k_unit_own, k_inverse_own)
    grad_proj = jnp.concatenate([grad_query, grad_key, grad_v_own], axis=-1)
    grad_proj = grad_proj.astype(jnp.bfloat16).reshape(-1, 3 * model_width)
    grad_in = lax.dot_general(
        grad_proj, w_qkv, (((1,), (1,)), ((), ())), preferred_element_type=jnp.float32
    )
    grad_features = grad_in.astype(jnp.bfloat16).reshape(tile_rows, tile_cols, model_width)
    qkv_term = lax.dot_general(
        flat_in, grad_proj, (((0,), (0,)), ((), ())), preferred_element_type=jnp.float32
    )
    scale_term = jnp.sum(scale_terms, axis=(1, 2))
    qkv_total, out_total, scale_total = lax.psum((qkv_term, out_term, scale_term), ("row", "col"))
    grad_norm = float(rows_all * cols_all) ** (-0.5)
    return (grad_features, qkv_total * grad_norm, out_total * grad_norm, scale_total * grad_norm)


def solution(mesh):
    placed = (P("row", "col", None), P("row", "col", None), P(), P(), P())
    return jax.shard_map(
        on_device,
        mesh=mesh,
        in_specs=placed,
        out_specs=(P("row", "col", None), P(), P(), P()),
        check_vma=False,
    )
```

profile of v0, /device:TPU:1, one launch (start us, length us, event | category | flops | bytes accessed | tf_op | source)
XLA Modules:
  0.0 889.7 jit_solution(2109987334469003675)
XLA Ops:
  9.0 8.8 collective-permute-start.1
  17.8 1.9 collective-permute-start
  28.7 1.3 collective-permute-start.3
  30.0 12.7 %collective-permute-start.2 = (bf16[14,3,256]{2,1,0:T(4,128)(2,1)S(1)}, bf16[14,3,256]{2,1,0:T(4,128)(2,1)S(1)}, u32[]{:S(2)}, u32[]{:S(2)}) collective-permute-start(bf16[14,3,256]{2,1,0:T(4,128)(2,1)S(1)} %get-tuple-element.1118), channel_id=1, source_target_pairs={{0,1},{1,2},{2,3},{3,4},{4,5},{5,6},{6,7},{7,8},{8,9},{9,10},{10,1... | collective-permute-start | bytes 64520 | tf_op jit(solution)/shard_map/ppermute | solution.py:24
  57.7 1.0 reshape.2679
  59.6 1.0 reshape.2678
  65.5 1.0 reshape.2675
  67.5 1.0 reshape.2674
  169.2 2.7 broadcast_multiply_fusion.2
  190.3 2.1 convolution_bitcast_fusion.1
  192.7 2.9 add_reduce_fusion
  217.1 1.2 fusion.67
  220.6 1.3 maximum_add_fusion
  221.9 1.8 scatter-add.191
  223.7 1.9 add_select_fusion.4
  225.7 1.6 scatter-add.194
  227.3 1.9 add_select_fusion.3
  229.2 1.5 scatter-add.195
  230.7 2.0 add_select_fusion.2
  232.7 1.5 scatter-add.196
  234.3 1.9 add_select_fusion.1
  236.2 1.5 scatter-add.199
  237.7 1.8 add_select_fusion
  239.6 1.5 scatter-add.200
  277.2 3.5 collective-permute-start.5
  280.8 2.0 collective-permute-start.4
  282.9 116.2 %psum.23 = f32[2]{0:T(128)S(1)} all-reduce(f32[2]{0:T(128)S(1)} %copy-done.233), channel_id=1, replica_groups=mesh['row'=16,'col'=32] {'row','col'}, use_global_device_ids=true, to_apply=%region_111.112 | all-reduce | flops 2 | bytes 16 | tf_op jit(solution)/shard_map/psum | solution.py:187
  399.2 1.3 collective-permute-start.7
  400.5 12.7 %collective-permute-start.6 = (bf16[20,3,256]{2,1,0:T(4,128)(2,1)S(1)}, bf16[20,3,256]{2,1,0:T(4,128)(2,1)S(1)}, u32[]{:S(2)}, u32[]{:S(2)}) collective-permute-start(bf16[20,3,256]{2,1,0:T(4,128)(2,1)S(1)} %get-tuple-element.1015), channel_id=1, source_target_pairs={{0,1},{1,2},{2,3},{3,4},{4,5},{5,6},{6,7},{7,8},{8,9},{9,10},{10,1... | collective-permute-start | bytes 92168 | tf_op jit(solution)/shard_map/ppermute | solution.py:24
  415.0 1.9 add_select_fusion.5
  416.9 1.4 scatter-add.280
  422.0 458.0 %all-reduce.4.cloned.1.call-done = (f32[128,384]{0,1:T(8,128)}, f32[128,128]{1,0:T(8,128)}) async-done(((f32[128,384]{0,1:T(8,128)}, f32[128,128]{1,0:T(8,128)}), (f32[128,384]{0,1:T(8,128)}, f32[128,128]{1,0:T(8,128)})) %all-reduce.4.cloned.1.call-update) | async-done | bytes 262160 | tf_op jit(solution)/shard_map/psum | solution.py:187
  (1279 shorter events, 214.8 us)
Async XLA Ops:
  7.2 872.8 %all-reduce.4.cloned.1.call-start = ((), (), s32[]{:S(2)}) async-start(), calls=%async_computation | async-start | bytes 524288 | tf_op jit(solution)/shard_map/psum | solution.py:187
  9.0 19.6 %collective-permute-start.1 = (bf16[3,16,256]{2,1,0:T(8,128)(2,1)S(1)}, bf16[3,16,256]{2,1,0:T(8,128)(2,1)S(1)}, u32[]{:S(2)}, u32[]{:S(2)}) collective-permute-start(bf16[3,16,256]{2,1,0:T(8,128)(2,1)S(1)} %get-tuple-element.1121), channel_id=1, source_target_pairs={{32,0},{64,32},{96,64},{128,96},{160,128},{192,160},{224,192},{256... | collective-permute-start | bytes 73736 | tf_op jit(solution)/shard_map/ppermute | solution.py:26
  17.8 10.8 %collective-permute-start = (bf16[3,16,256]{2,1,0:T(8,128)(2,1)S(1)}, bf16[3,16,256]{2,1,0:T(8,128)(2,1)S(1)}, u32[]{:S(2)}, u32[]{:S(2)}) collective-permute-start(bf16[3,16,256]{2,1,0:T(8,128)(2,1)S(1)} %get-tuple-element.1120), channel_id=1, source_target_pairs={{0,32},{32,64},{64,96},{96,128},{128,160},{160,192},{192,224},{224... | collective-permute-start | bytes 73736 | tf_op jit(solution)/shard_map/ppermute | solution.py:24
  28.7 14.6 %collective-permute-start.3 = (bf16[14,3,256]{2,1,0:T(4,128)(2,1)S(1)}, bf16[14,3,256]{2,1,0:T(4,128)(2,1)S(1)}, u32[]{:S(2)}, u32[]{:S(2)}) collective-permute-start(bf16[14,3,256]{2,1,0:T(4,128)(2,1)S(1)} %get-tuple-element.1119), channel_id=1, source_target_pairs={{1,0},{2,1},{3,2},{4,3},{5,4},{6,5},{7,6},{8,7},{9,8},{10,9},{11,1... | collective-permute-start | bytes 64520 | tf_op jit(solution)/shard_map/ppermute | solution.py:26
  30.0 13.7 %collective-permute-start.2 = (bf16[14,3,256]{2,1,0:T(4,128)(2,1)S(1)}, bf16[14,3,256]{2,1,0:T(4,128)(2,1)S(1)}, u32[]{:S(2)}, u32[]{:S(2)}) collective-permute-start(bf16[14,3,256]{2,1,0:T(4,128)(2,1)S(1)} %get-tuple-element.1118), channel_id=1, source_target_pairs={{0,1},{1,2},{2,3},{3,4},{4,5},{5,6},{6,7},{7,8},{8,9},{9,10},{10,1... | collective-permute-start | bytes 64520 | tf_op jit(solution)/shard_map/ppermute | solution.py:24
  59.6 112.3 %copy-start.109 = (f32[8,16]{1,0:T(8,128)}, f32[8,16]{1,0:T(8,128)S(1)}, u32[]{:S(2)}) copy-start(f32[8,16]{1,0:T(8,128)S(1)} %get-tuple-element.804) | copy-start | bytes 1540
  81.6 94.5 %copy-start.134 = (f32[8,16]{1,0:T(8,128)}, f32[8,16]{1,0:T(8,128)S(1)}, u32[]{:S(2)}) copy-start(f32[8,16]{1,0:T(8,128)S(1)} %get-tuple-element.780) | copy-start | bytes 1540
  81.6 94.5 %copy-start.136 = (f32[8,16]{1,0:T(8,128)}, f32[8,16]{1,0:T(8,128)S(1)}, u32[]{:S(2)}) copy-start(f32[8,16]{1,0:T(8,128)S(1)} %get-tuple-element.781) | copy-start | bytes 1540
  82.2 94.0 %copy-start.138 = (f32[8,16]{1,0:T(8,128)}, f32[8,16]{1,0:T(8,128)S(1)}, u32[]{:S(2)}) copy-start(f32[8,16]{1,0:T(8,128)S(1)} %get-tuple-element.778) | copy-start | bytes 1540
  82.2 94.0 %copy-start.140 = (f32[8,16]{1,0:T(8,128)}, f32[8,16]{1,0:T(8,128)S(1)}, u32[]{:S(2)}) copy-start(f32[8,16]{1,0:T(8,128)S(1)} %get-tuple-element.779) | copy-start | bytes 1540
  82.7 93.5 %copy-start.142 = (f32[8,16]{1,0:T(8,128)}, f32[8,16]{1,0:T(8,128)S(1)}, u32[]{:S(2)}) copy-start(f32[8,16]{1,0:T(8,128)S(1)} %get-tuple-element.776) | copy-start | bytes 1540
  82.7 93.5 %copy-start.144 = (f32[8,16]{1,0:T(8,128)}, f32[8,16]{1,0:T(8,128)S(1)}, u32[]{:S(2)}) copy-start(f32[8,16]{1,0:T(8,128)S(1)} %get-tuple-element.777) | copy-start | bytes 1540
  83.2 93.2 %copy-start.146 = (f32[8,16]{1,0:T(8,128)}, f32[8,16]{1,0:T(8,128)S(1)}, u32[]{:S(2)}) copy-start(f32[8,16]{1,0:T(8,128)S(1)} %get-tuple-element.774) | copy-start | bytes 1540
  83.3 93.2 %copy-start.148 = (f32[8,16]{1,0:T(8,128)}, f32[8,16]{1,0:T(8,128)S(1)}, u32[]{:S(2)}) copy-start(f32[8,16]{1,0:T(8,128)S(1)} %get-tuple-element.775) | copy-start | bytes 1540
  83.8 92.7 %copy-start.150 = (f32[8,16]{1,0:T(8,128)}, f32[8,16]{1,0:T(8,128)S(1)}, u32[]{:S(2)}) copy-start(f32[8,16]{1,0:T(8,128)S(1)} %get-tuple-element.772) | copy-start | bytes 1540
  83.8 92.7 %copy-start.152 = (f32[8,16]{1,0:T(8,128)}, f32[8,16]{1,0:T(8,128)S(1)}, u32[]{:S(2)}) copy-start(f32[8,16]{1,0:T(8,128)S(1)} %get-tuple-element.773) | copy-start | bytes 1540
  84.3 92.2 %copy-start.154 = (f32[8,16]{1,0:T(8,128)}, f32[8,16]{1,0:T(8,128)S(1)}, u32[]{:S(2)}) copy-start(f32[8,16]{1,0:T(8,128)S(1)} %get-tuple-element.770) | copy-start | bytes 1540
  84.3 92.2 %copy-start.156 = (f32[8,16]{1,0:T(8,128)}, f32[8,16]{1,0:T(8,128)S(1)}, u32[]{:S(2)}) copy-start(f32[8,16]{1,0:T(8,128)S(1)} %get-tuple-element.771) | copy-start | bytes 1540
  84.9 91.7 %copy-start.158 = (f32[8,16]{1,0:T(8,128)}, f32[8,16]{1,0:T(8,128)S(1)}, u32[]{:S(2)}) copy-start(f32[8,16]{1,0:T(8,128)S(1)} %get-tuple-element.768) | copy-start | bytes 1540
  84.9 91.7 %copy-start.160 = (f32[8,16]{1,0:T(8,128)}, f32[8,16]{1,0:T(8,128)S(1)}, u32[]{:S(2)}) copy-start(f32[8,16]{1,0:T(8,128)S(1)} %get-tuple-element.769) | copy-start | bytes 1540
  85.4 91.3 %copy-start.162 = (f32[8,16]{1,0:T(8,128)}, f32[8,16]{1,0:T(8,128)S(1)}, u32[]{:S(2)}) copy-start(f32[8,16]{1,0:T(8,128)S(1)} %get-tuple-element.766) | copy-start | bytes 1540
  85.4 91.3 %copy-start.164 = (f32[8,16]{1,0:T(8,128)}, f32[8,16]{1,0:T(8,128)S(1)}, u32[]{:S(2)}) copy-start(f32[8,16]{1,0:T(8,128)S(1)} %get-tuple-element.767) | copy-start | bytes 1540
  86.0 90.7 %copy-start.166 = (f32[8,16]{1,0:T(8,128)}, f32[8,16]{1,0:T(8,128)S(1)}, u32[]{:S(2)}) copy-start(f32[8,16]{1,0:T(8,128)S(1)} %get-tuple-element.764) | copy-start | bytes 1540
  86.0 90.7 %copy-start.168 = (f32[8,16]{1,0:T(8,128)}, f32[8,16]{1,0:T(8,128)S(1)}, u32[]{:S(2)}) copy-start(f32[8,16]{1,0:T(8,128)S(1)} %get-tuple-element.765) | copy-start | bytes 1540
  86.5 90.2 %copy-start.170 = (f32[8,16]{1,0:T(8,128)}, f32[8,16]{1,0:T(8,128)S(1)}, u32[]{:S(2)}) copy-start(f32[8,16]{1,0:T(8,128)S(1)} %get-tuple-element.762) | copy-start | bytes 1540
  86.5 90.2 %copy-start.172 = (f32[8,16]{1,0:T(8,128)}, f32[8,16]{1,0:T(8,128)S(1)}, u32[]{:S(2)}) copy-start(f32[8,16]{1,0:T(8,128)S(1)} %get-tuple-element.763) | copy-start | bytes 1540
  87.0 89.7 %copy-start.174 = (f32[8,16]{1,0:T(8,128)}, f32[8,16]{1,0:T(8,128)S(1)}, u32[]{:S(2)}) copy-start(f32[8,16]{1,0:T(8,128)S(1)} %get-tuple-element.760) | copy-start | bytes 1540
  87.1 89.7 %copy-start.176 = (f32[8,16]{1,0:T(8,128)}, f32[8,16]{1,0:T(8,128)S(1)}, u32[]{:S(2)}) copy-start(f32[8,16]{1,0:T(8,128)S(1)} %get-tuple-element.761) | copy-start | bytes 1540
  277.2 121.9 %collective-permute-start.5 = (bf16[3,22,256]{2,1,0:T(8,128)(2,1)S(1)}, bf16[3,22,256]{2,1,0:T(8,128)(2,1)S(1)}, u32[]{:S(2)}, u32[]{:S(2)}) collective-permute-start(bf16[3,22,256]{2,1,0:T(8,128)(2,1)S(1)} %get-tuple-element.1117), channel_id=1, source_target_pairs={{32,0},{64,32},{96,64},{128,96},{160,128},{192,160},{224,192},{256... | collective-permute-start | bytes 101384 | tf_op jit(solution)/shard_map/ppermute | solution.py:26
  280.8 118.3 %collective-permute-start.4 = (bf16[3,22,256]{2,1,0:T(8,128)(2,1)S(1)}, bf16[3,22,256]{2,1,0:T(8,128)(2,1)S(1)}, u32[]{:S(2)}, u32[]{:S(2)}) collective-permute-start(bf16[3,22,256]{2,1,0:T(8,128)(2,1)S(1)} %get-tuple-element.1116), channel_id=1, source_target_pairs={{0,32},{32,64},{64,96},{96,128},{128,160},{160,192},{192,224},{224... | collective-permute-start | bytes 101384 | tf_op jit(solution)/shard_map/ppermute | solution.py:24
  399.2 14.5 %collective-permute-start.7 = (bf16[20,3,256]{2,1,0:T(4,128)(2,1)S(1)}, bf16[20,3,256]{2,1,0:T(4,128)(2,1)S(1)}, u32[]{:S(2)}, u32[]{:S(2)}) collective-permute-start(bf16[20,3,256]{2,1,0:T(4,128)(2,1)S(1)} %get-tuple-element.1016), channel_id=1, source_target_pairs={{1,0},{2,1},{3,2},{4,3},{5,4},{6,5},{7,6},{8,7},{9,8},{10,9},{11,1... | collective-permute-start | bytes 92168 | tf_op jit(solution)/shard_map/ppermute | solution.py:26
  400.5 13.8 %collective-permute-start.6 = (bf16[20,3,256]{2,1,0:T(4,128)(2,1)S(1)}, bf16[20,3,256]{2,1,0:T(4,128)(2,1)S(1)}, u32[]{:S(2)}, u32[]{:S(2)}) collective-permute-start(bf16[20,3,256]{2,1,0:T(4,128)(2,1)S(1)} %get-tuple-element.1015), channel_id=1, source_target_pairs={{0,1},{1,2},{2,3},{3,4},{4,5},{5,6},{6,7},{7,8},{8,9},{9,10},{10,1... | collective-permute-start | bytes 92168 | tf_op jit(solution)/shard_map/ppermute | solution.py:24
  (213 other events, 1629.6 us)
Sparse Core Ops, SparseCore 0:
  421.3 458.5 all-reduce.3
where the time goes:
time: 906 us; the launch traced here: 890 us
  waiting for transfers between devices  459 us (51%)
  local copies, waits for them, and re-layouts  165 us (18%)
  blocking collectives  116 us (13%)
  other arithmetic  80.2 us (9%)
  starting transfers between devices  44.3 us (5%)
  between operations  20.3 us (2%)
    psum x1, waiting for transfers between devices, on_device(): lax.psum((qkv_term, out_term, scale_term), ('row', 'col'))  458 us
    psum x1, blocking collectives, on_device(): lax.psum((qkv_term, out_term, scale_term), ('row', 'col'))  116 us
    slice x102, local copies, waits for them, and re-layouts, head_sums(): return jnp.stack([totals[:, :, head] for head in range(HEADS)], axis=0)  63.5 us
    unnamed x474, local copies, waits for them, and re-layouts  33.8 us
    ppermute x4, starting transfers between devices, extended(): lax.ppermute(tail, axis, [(i, (i + 1) % count) for i in range(ends)])  29.4 us
    reshape x102, local copies, waits for them, and re-layouts, head_sums(): product = (left * right).reshape(left.shape[:2] + (HEADS, HEAD_DIM))  23 us
    reduce_sum x102, other arithmetic, head_sums(): totals = jnp.sum(product, axis=-1)  21.8 us
    scatter-add x42, local copies, waits for them, and re-layouts, window_pass(): grad_kv = grad_kv.at[shift_row:shift_row + out_rows, shift_col:shift_col...  18.5 us
  transfers between devices with their start and end apart: 9, of which 3 were waited for; matrix products, arithmetic and copies ran while one was open for 1% of the time, Pallas kernels for 0%

commit v1 on v0

v1 whole, which is shorter than its diff:
```python
import functools

import jax
import jax.numpy as jnp
import numpy as np
from jax import lax
from jax.experimental import pallas as pl
from jax.experimental.pallas import tpu as pltpu
from jax.sharding import Mesh
from jax.sharding import PartitionSpec as P

RADIUS = 3
EPSILON = 1e-06
MODEL = 128
HEAD = 64
ROWS, COLS = 8, 16
OWN = ROWS * COLS
QUERIES = 352
KEYS = 640
NEAR = 384
BLOCK = 32
SHARES = 32
LOG2E = 1.4426950408889634
FAR_AWAY = 1e4

F32 = jnp.float32
BF16 = jnp.bfloat16


def side_columns(left, inner):
    if left:
        return -3 if inner else -6
    return 16 if inner else 19


def token_table(core):
    def tile(holder, start, count, lift):
        token = start + np.arange(count)
        return np.stack([8 * holder + token // 16 + lift, token % 16])

    def edge(start, count, left, inner, lift):
        token = start + np.arange(count)
        return np.stack([token // 3 + lift, token % 3 + side_columns(left, inner)])

    other = 1 - core
    lift = -16 if core == 0 else 16
    far_left = core == 0
    sent_left = other == 0
    pieces = [
        tile(core, 0, 128, 0),
        tile(other, 80 * core, 48, 0),
        edge(0, 48, far_left, True, 0),
        edge(0, 48, not far_left, True, 0),
        tile(other, 80 * other, 48, lift),
        edge(32 * other, 16, sent_left, True, lift),
        edge(32 * other, 16, not sent_left, True, lift),
        tile(other, 48 - 16 * core, 48, 0),
        edge(0, 48, far_left, False, 0),
        edge(0, 48, not far_left, False, 0),
        tile(other, 48 - 16 * other, 48, lift),
        edge(16, 16, sent_left, True, lift),
        edge(16 * other, 32, sent_left, False, lift),
        edge(16, 16, not sent_left, True, lift),
        edge(16 * other, 32, not sent_left, False, lift),
    ]
    return np.concatenate(pieces, axis=1).astype(np.float32)


TABLES = np.stack([token_table(0), token_table(1)])


def vmem(count):
    return [pl.BlockSpec(memory_space=pltpu.VMEM)] * count


def dot_nt(left, right):
    return lax.dot_general(
        left, right, (((1,), (1,)), ((), ())), preferred_element_type=F32
    )


def dot_tn(left, right):
    return lax.dot_general(
        left, right, (((0,), (0,)), ((), ())), preferred_element_type=F32
    )


def dot_nn(left, right):
    return jnp.dot(left, right, preferred_element_type=F32)


def far_kernel(place, feat, cot, other_feat, other_cot, out):
    core = place[0]
    spot = lax.broadcasted_iota(jnp.int32, (96, 128), 0)
    token = lax.broadcasted_iota(jnp.int32, (96, 128), 1)
    outer = jnp.where(spot >= 48, 1, 0)
    index = spot - 48 * outer
    row = (index * 43) >> 7
    step = index - 3 * row
    column = step + jnp.where(core == 0, 13 - 3 * outer, 3 * outer)
    half = row >> 3
    wanted = (row - 8 * half) * 16 + column
    mine = jnp.where((wanted == token) & (half == core), 1.0, 0.0).astype(BF16)
    theirs = jnp.where((wanted == token) & (half != core), 1.0, 0.0).astype(BF16)
    out[0:96, :] = (dot_nn(mine, feat[...]) + dot_nn(theirs, other_feat[...])).astype(BF16)
    out[96:144, :] = (
        dot_nn(mine[0:48], cot[...]) + dot_nn(theirs[0:48], other_cot[...])
    ).astype(BF16)


def rows_at(ref, start, count):
    return ref[pl.ds(pl.multiple_of(start, 16), count), :]


def vertical_kernel(place, feat, cot, far, swapped, out):
    core = place[0]
    out[0:48, :] = rows_at(feat, 80 * core, 48)
    out[48:64, :] = rows_at(far, 32 * core, 16)
    out[64:80, :] = rows_at(swapped, 32 * core, 16)
    out[80:128, :] = rows_at(feat, 48 - 16 * core, 48)
    out[128:144, :] = far[16:32, :]
    out[144:176, :] = rows_at(far, 48 + 16 * core, 32)
    out[176:192, :] = swapped[16:32, :]
    out[192:224, :] = rows_at(swapped, 48 + 16 * core, 32)
    out[224:272, :] = rows_at(cot, 80 * core, 48)
    out[272:288, :] = rows_at(far, 96 + 32 * core, 16)
    out[288:304, :] = rows_at(swapped, 96 + 32 * core, 16)


def attention_kernel(
    place,
    cos_scale,
    feat,
    cot,
    other_feat,
    other_cot,
    far,
    swapped,
    vertical,
    w_qkv,
    w_out,
    key_spots,
    query_spots,
    grad_feat,
    grad_w,
    grad_scale,
    tokens,
    cots,
    keys,
    values,
    queries,
    d_attn,
    raw,
    dots,
    bias,
    mix_own,
    mix_key,
    slope_own,
    slope_key,
):
    core = place[0]
    tokens[0:128, :] = feat[...]
    tokens[128:176, :] = rows_at(other_feat, 80 * core, 48)
    tokens[176:224, :] = far[0:48, :]
    tokens[224:272, :] = swapped[0:48, :]
    tokens[272:352, :] = vertical[0:80, :]
    tokens[352:400, :] = rows_at(other_feat, 48 - 16 * core, 48)
    tokens[400:448, :] = far[48:96, :]
    tokens[448:496, :] = swapped[48:96, :]
    tokens[496:640, :] = vertical[80:224, :]
    cots[0:128, :] = cot[...]
    cots[128:176, :] = rows_at(other_cot, 80 * core, 48)
    cots[176:224, :] = far[96:144, :]
    cots[224:272, :] = swapped[96:144, :]
    cots[272:352, :] = vertical[224:304, :]

    keys[...] = dot_nn(tokens[...], w_qkv[:, MODEL : 2 * MODEL]).astype(BF16)
    values[...] = dot_nn(tokens[...], w_qkv[:, 2 * MODEL :]).astype(BF16)
    queries[...] = dot_nn(tokens[0:QUERIES, :], w_qkv[:, :MODEL]).astype(BF16)
    d_attn[...] = dot_nt(cots[...], w_out[...]).astype(BF16)

    spots = key_spots[pl.ds(core, 1)].reshape(8, KEYS)
    key_rows, key_cols = spots[0:1, :], spots[1:2, :]
    all_rows = key_rows + place[1].astype(F32)
    all_cols = key_cols + place[2].astype(F32)
    inside = (all_rows >= 0) & (all_rows < 128) & (all_cols >= 0) & (all_cols < 512)
    key_rows = jnp.where(inside, key_rows, FAR_AWAY)
    for start in range(0, QUERIES, BLOCK):
        here = query_spots[pl.ds(core, 1), start : start + BLOCK, :].reshape(BLOCK, 8)
        apart = jnp.maximum(
            jnp.abs(here[:, 0:1] - key_rows), jnp.abs(here[:, 1:2] - key_cols)
        )
        bias[start : start + BLOCK, :] = jnp.where(apart <= RADIUS, 0.0, -1e30)

    key_wide = keys[...].astype(F32)
    square = key_wide * key_wide
    upper = square.astype(BF16)
    lower = (square - upper.astype(F32)).astype(BF16)
    head_of = lax.broadcasted_iota(jnp.int32, (16, MODEL), 1) // HEAD
    picks = jnp.where(
        head_of == lax.broadcasted_iota(jnp.int32, (16, MODEL), 0), 1.0, 0.0
    ).astype(BF16)
    key_inverse = lax.rsqrt(dot_nt(picks, upper) + dot_nt(picks, lower) + EPSILON)

    first = lax.broadcasted_iota(jnp.int32, (1, MODEL), 1) < HEAD

    def head_sums(array):
        low = jnp.sum(jnp.where(first, array, 0.0), axis=1, keepdims=True)
        high = jnp.sum(jnp.where(first, 0.0, array), axis=1, keepdims=True)
        return low, high

    for head in range(2):
        own_lanes = first if head == 0 else ~first
        raw[head] = dot_nt(jnp.where(own_lanes, queries[...], 0.0).astype(BF16), keys[...])
        dots[head] = dot_nt(jnp.where(own_lanes, d_attn[...], 0.0).astype(BF16), values[...])

    scale_sums = [jnp.zeros((BLOCK, 1), F32), jnp.zeros((BLOCK, 1), F32)]
    for start in range(0, QUERIES, BLOCK):
        rows = slice(start, start + BLOCK)
        query_wide = queries[rows, :].astype(F32)
        norms = head_sums(query_wide * query_wide)
        for head in range(2):
            inverse = lax.rsqrt(norms[head] + EPSILON)
            reach = inverse * cos_scale[head]
            key_inv = key_inverse[head : head + 1, :]
            score = raw[head, rows, :] * (reach * LOG2E) * key_inv + bias[rows, :]
            expo = jnp.exp2(score)
            gain = dots[head, rows, :]
            share = 1.0 / (jnp.sum(expo, axis=1, keepdims=True) + 1e-30)
            center = jnp.sum(expo * gain, axis=1, keepdims=True) * share
            if start < OWN:
                weight = expo[:, :NEAR] * share
                slope = weight * (gain[:, :NEAR] - center)
                pull = slope * key_inv[:, :NEAR]
                scale_sums[head] += inverse * jnp.sum(
                    pull * raw[head, rows, :NEAR], axis=1, keepdims=True
                )
                mix_own[head, rows, :] = weight.astype(BF16)
                slope_own[head, rows, :] = (pull * cos_scale[head]).astype(BF16)
                weight = weight[:, :OWN]
                slope = slope[:, :OWN]
            else:
                weight = expo[:, :OWN] * share
                slope = weight * (gain[:, :OWN] - center)
            mix_key[head, rows, :] = weight.astype(BF16)
            slope_key[head, rows, :] = (slope * reach).astype(BF16)

    def both(dot, left, right):
        return jnp.where(first, dot(left[0], right), dot(left[1], right))

    attn_out = both(dot_nn, mix_own, values[0:NEAR, :]).astype(BF16)
    dq_unit = both(dot_nn, slope_own, keys[0:NEAR, :])
    dk_unit = both(dot_tn, slope_key, queries[...])
    dv = both(dot_tn, mix_key, d_attn[...])

    def unit_backward(vector, grad_unit):
        low, high = head_sums(vector * vector)
        inverse = jnp.where(first, lax.rsqrt(low + EPSILON), lax.rsqrt(high + EPSILON))
        unit = vector * inverse
        low, high = head_sums(unit * grad_unit)
        return (grad_unit - unit * jnp.where(first, low, high)) * inverse

    dq = unit_backward(queries[0:OWN, :].astype(F32), dq_unit).astype(BF16)
    dk = unit_backward(keys[0:OWN, :].astype(F32), dk_unit).astype(BF16)
    dv = dv.astype(BF16)
    grad_feat[...] = (
        dot_nt(dq, w_qkv[:, :MODEL])
        + dot_nt(dk, w_qkv[:, MODEL : 2 * MODEL])
        + dot_nt(dv, w_qkv[:, 2 * MODEL :])
    ).astype(BF16)
    norm = 1.0 / 256.0
    for part, grad in enumerate((dq, dk, dv)):
        grad_w[part * MODEL : (part + 1) * MODEL, :] = (
            dot_tn(feat[...], grad) * norm
        ).astype(BF16)
    grad_w[3 * MODEL :, :] = (dot_tn(attn_out, cot[...]) * norm).astype(BF16)

    lane = lax.broadcasted_iota(jnp.int32, (8, MODEL), 1)
    held = jnp.zeros((8, MODEL), F32)
    for head in range(2):
        rest = jnp.sum(scale_sums[head], axis=0, keepdims=True) * norm
        for part in range(3):
            piece = rest.astype(BF16).astype(F32)
            held = jnp.where(lane == 3 * head + part, piece, held)
            rest = rest - piece
    grad_scale[...] = held.astype(BF16)


def pairs(target):
    found = []
    for row in range(16):
        for col in range(32):
            to_row, to_col = target(row, col)
            if 0 <= to_row < 16 and 0 <= to_col < 32:
                found.append((row * 32 + col, to_row * 32 + to_col))
    return found


EVERY = ("lo", "core", "x", "y", "hi")
PLANE = ("x", "y", "core")
LINE = ("lo", "hi")
CHIP_MATE = pairs(lambda row, col: (row ^ 1, col))
FAR_MATE = pairs(lambda row, col: (row, col - 1 if row % 2 else col + 1))
NEXT_CHIP = pairs(lambda row, col: (row + 1 if row % 2 else row - 1, col))


def exchange(array, axes):
    return lax.all_to_all(array, axes, 0, 0, tiled=True)


def to_all(array, axes, count):
    return exchange(jnp.broadcast_to(array[None], (count,) + array.shape), axes)


def on_device(features, cotangent, w_qkv, w_out, cos_scale):
    core = lax.axis_index("core")
    col = lax.axis_index(("x", "y", "hi"))
    place = jnp.stack([core, lax.axis_index("lo") * 16, col * 16]).astype(jnp.int32)
    feat = features.reshape(OWN, MODEL)
    cot = cotangent.reshape(OWN, MODEL)
    smem = pl.BlockSpec(memory_space=pltpu.SMEM)

    other = lax.ppermute(jnp.stack([feat, cot]), EVERY, CHIP_MATE)
    other_feat, other_cot = other[0], other[1]
    far_out = pl.pallas_call(
        far_kernel,
        out_shape=jax.ShapeDtypeStruct((144, MODEL), BF16),
        in_specs=[smem] + vmem(4),
        out_specs=vmem(1)[0],
        name="far_edges",
    )(place, feat, cot, other_feat, other_cot)
    far = lax.ppermute(far_out, EVERY, FAR_MATE)
    swapped = lax.ppermute(far, EVERY, CHIP_MATE)
    vertical_out = pl.pallas_call(
        vertical_kernel,
        out_shape=jax.ShapeDtypeStruct((304, MODEL), BF16),
        in_specs=[smem] + vmem(4),
        out_specs=vmem(1)[0],
        name="vertical_edges",
    )(place, feat, cot, far, swapped)
    vertical = lax.ppermute(vertical_out, EVERY, NEXT_CHIP)

    key_spots = np.zeros((2, 8, KEYS), np.float32)
    key_spots[:, :2] = TABLES
    query_spots = np.zeros((2, QUERIES, 8), np.float32)
    query_spots[:, :, :2] = TABLES[:, :, :QUERIES].transpose(0, 2, 1)
    grad_feat, grad_w, scale_tile = pl.pallas_call(
        attention_kernel,
        out_shape=(
            jax.ShapeDtypeStruct((OWN, MODEL), BF16),
            jax.ShapeDtypeStruct((4 * MODEL, MODEL), BF16),
            jax.ShapeDtypeStruct((8, MODEL), BF16),
        ),
        in_specs=[smem, smem] + vmem(11),
        out_specs=vmem(3),
        scratch_shapes=[
            pltpu.VMEM((KEYS, MODEL), BF16),
            pltpu.VMEM((QUERIES, MODEL), BF16),
            pltpu.VMEM((KEYS, MODEL), BF16),
            pltpu.VMEM((KEYS, MODEL), BF16),
            pltpu.VMEM((QUERIES, MODEL), BF16),
            pltpu.VMEM((QUERIES, MODEL), BF16),
            pltpu.VMEM((2, QUERIES, KEYS), F32),
            pltpu.VMEM((2, QUERIES, KEYS), F32),
            pltpu.VMEM((QUERIES, KEYS), F32),
            pltpu.VMEM((2, OWN, NEAR), BF16),
            pltpu.VMEM((2, QUERIES, OWN), BF16),
            pltpu.VMEM((2, OWN, NEAR), BF16),
            pltpu.VMEM((2, QUERIES, OWN), BF16),
        ],
        compiler_params=pltpu.CompilerParams(vmem_limit_bytes=32 * 1024 * 1024),
        name="window_attention",
    )(
        place,
        cos_scale,
        feat,
        cot,
        other_feat,
        other_cot,
        far,
        swapped,
        vertical,
        w_qkv,
        w_out,
        jnp.asarray(key_spots),
        jnp.asarray(query_spots),
    )

    scale_rows = jnp.broadcast_to(scale_tile[None], (SHARES, 8, MODEL))
    shares = jnp.concatenate([grad_w.reshape(SHARES, 16, MODEL), scale_rows], axis=1)
    share = jnp.sum(exchange(shares, PLANE).astype(F32), axis=0)
    pieces = share[16:17, 0:6].reshape(2, 3)
    scale_part = jnp.sum(pieces, axis=1, keepdims=True)
    top = lax.reduce_precision(scale_part, 8, 7)
    middle = lax.reduce_precision(scale_part - top, 8, 7)
    split = jnp.concatenate([top, middle, scale_part - top - middle], axis=1)
    split = jnp.pad(split.reshape(1, 6), ((0, 7), (0, MODEL - 6)))
    share = jnp.concatenate([share[:16], split], axis=0).astype(BF16)
    share = jnp.sum(to_all(share, LINE, 16).astype(F32), axis=0)
    grad_scale = jnp.sum(share[16, 0:6].reshape(2, 3), axis=1)
    whole = to_all(share[:16].astype(BF16), PLANE, SHARES).astype(F32)
    whole = whole.reshape(4, MODEL, MODEL)
    grad_w_qkv = jnp.concatenate([whole[0], whole[1], whole[2]], axis=1)
    return (grad_feat.reshape(ROWS, COLS, MODEL), grad_w_qkv, whole[3], grad_scale)


def solution(mesh):
    fine = Mesh(mesh.devices.reshape(8, 2, 4, 4, 2), EVERY)
    tokens = P(("lo", "core"), ("x", "y", "hi"), None)
    return jax.shard_map(
        on_device,
        mesh=fine,
        in_specs=(tokens, tokens, P(), P(), P()),
        out_specs=(tokens, P(), P(), P()),
        check_vma=False,
    )
```

time: 906 us -> 100 us (0.11); the launches traced: 890 us -> 99.6 us
  waiting for transfers between devices: 459 us -> 24.8 us
  local copies, waits for them, and re-layouts: 165 us -> 4.58 us
  other arithmetic: 80.2 us -> 3.04 us
  blocking collectives: 116 us -> 40.4 us
  starting transfers between devices: 44.3 us -> 19.6 us
  between operations: 20.3 us -> 0.85 us
    psum x1 -> x0, waiting for transfers between devices: 458 us -> none  [on_device(): lax.psum((qkv_term, out_term, scale_term), ('row', 'col'))]
    psum x1 -> x0, blocking collectives: 116 us -> none  [on_device(): lax.psum((qkv_term, out_term, scale_term), ('row', 'col'))]
    slice x112 -> x5, local copies, waits for them, and re-layouts: 65.8 us -> 0.7 us  [the longest x1 0.65 us: on_device(): whole[3]]
    all_to_all x0 -> x2, blocking collectives: none -> 40.4 us  [exchange(): return lax.all_to_all(array, axes, 0, 0, tiled=True)]
    mul x57 -> x0, other arithmetic: 38.8 us -> none  [the longest x16 13 us: window_pass(): scaled * q_unit]
    unnamed x474 -> x28, local copies, waits for them, and re-layouts: 33.8 us -> 2.19 us
    ppermute x8 -> x4, starting transfers between devices: 44.3 us -> 14 us  [the longest x1 8.77 us: on_device(): other = lax.ppermute(jnp.stack([feat, cot]), EVERY, CHIP_MATE)]
    reduce_sum x103 -> x4, other arithmetic: 24.7 us -> 0.81 us  [the longest x1 0.63 us: on_device(): grad_scale = jnp.sum(share[16, 0:6].reshape(2, 3), axis=1)]
  transfers between devices with their start and end apart: 9 -> 5, of which waited for: 3 -> 5; matrix products, arithmetic and copies ran while one was open for 1% -> 1% of each run, Pallas kernels for 0% -> 0%
where the time goes in v1:
time: 100 us; the launch traced here: 99.6 us
  blocking collectives  40.4 us (40%)
  waiting for transfers between devices  24.8 us (25%)
  starting transfers between devices  19.6 us (20%)
  Pallas kernels  6.27 us (6%)
  local copies, waits for them, and re-layouts  4.58 us (5%)
  other arithmetic  3.04 us (3%)
    all_to_all x2, blocking collectives, exchange(): return lax.all_to_all(array, axes, 0, 0, tiled=True)  40.4 us
    ppermute x1, waiting for transfers between devices, on_device(): far = lax.ppermute(far_out, EVERY, FAR_MATE)  12.3 us
    ppermute x1, starting transfers between devices, on_device(): other = lax.ppermute(jnp.stack([feat, cot]), EVERY, CHIP_MATE)  8.77 us
    all_to_all x1, waiting for transfers between devices, exchange(): return lax.all_to_all(array, axes, 0, 0, tiled=True)  7.08 us
    all_to_all x1, starting transfers between devices, exchange(): return lax.all_to_all(array, axes, 0, 0, tiled=True)  5.62 us
    ppermute x1, waiting for transfers between devices, on_device(): vertical = lax.ppermute(vertical_out, EVERY, NEXT_CHIP)  4 us
    pallas_call x1, Pallas kernels, on_device(): pl.pallas_call(attention_kernel, out_shape=(jax.ShapeDtypeStruct((OWN, MO...  3.16 us
    unnamed x28, local copies, waits for them, and re-layouts  2.19 us
  transfers between devices with their start and end apart: 5, of which 5 were waited for; matrix products, arithmetic and copies ran while one was open for 1% of the time, Pallas kernels for 0%

profile of v1, /device:TPU:1, one launch (start us, length us, event | category | flops | bytes accessed | tf_op | source)
XLA Modules:
  0.0 99.6 jit_solution(3562969594380805333)
XLA Ops:
  0.6 0.0 copy-start.2
  0.6 0.8 pad_maximum_fusion.2
  1.5 8.8 %collective-permute-start = (bf16[2,128,128]{2,1,0:T(8,128)(2,1)S(1)}, bf16[2,128,128]{2,1,0:T(8,128)(2,1)S(1)}, u32[]{:S(2)}, u32[]{:S(2)}) collective-permute-start(bf16[2,128,128]{2,1,0:T(8,128)(2,1)S(1)} %pad_maximum_fusion.2), channel_id=1, source_target_pairs={{0,32},{1,33},{2,34},{3,35},{4,36},{5,37},{6,38},{7,39},{8,40},{9,... | collective-permute-start | bytes 196616 | tf_op jit(solution)/shard_map/ppermute | solution.py:323
  10.3 0.7 pad_add_fusion.place
  10.9 0.2 collective-permute-done
  11.1 0.6 slice_bitcast_fusion
  11.8 1.6 %far_edges.1 = bf16[144,128]{1,0:T(8,128)(2,1)} custom-call(s32[3]{0:T(128)} %pad_add_fusion.place, bf16[128,128]{1,0:T(8,128)(2,1)} %bitcast.25, bf16[128,128]{1,0:T(8,128)(2,1)} %bitcast.29, bf16[128,128]{1,0:T(8,128)(2,1)} %get-tuple-element.15.other_feat, bf16[128,128]{1,0:T(8,128)(2,1)} %get-tuple-element.14.other_cot), custom_call_target="tpu_custom_call" | custom-call | tf_op jit(solution)/shard_map/far_edges/pallas_call | solution.py:325
  13.4 0.0 copy-start.10
  13.5 1.4 %collective-permute-start.1 = (bf16[144,128]{1,0:T(8,128)(2,1)}, bf16[144,128]{1,0:T(8,128)(2,1)S(1)}, u32[]{:S(2)}, u32[]{:S(2)}) collective-permute-start(bf16[144,128]{1,0:T(8,128)(2,1)} %far_edges.1), channel_id=1, source_target_pairs={{0,1},{1,2},{2,3},{3,4},{4,5},{5,6},{6,7},{7,8},{8,9},{9,10},{10,1... | collective-permute-start | bytes 110600 | tf_op jit(solution)/shard_map/ppermute | solution.py:332
  14.9 12.3 %collective-permute-done.1.far = bf16[144,128]{1,0:T(8,128)(2,1)S(1)} collective-permute-done((bf16[144,128]{1,0:T(8,128)(2,1)}, bf16[144,128]{1,0:T(8,128)(2,1)S(1)}, u32[]{:S(2)}, u32[]{:S(2)}) %collective-permute-start.1) | collective-permute-done | bytes 36896 | tf_op jit(solution)/shard_map/ppermute | solution.py:332
  27.2 1.9 %collective-permute-start.2 = (bf16[144,128]{1,0:T(8,128)(2,1)S(1)}, bf16[144,128]{1,0:T(8,128)(2,1)S(1)}, u32[]{:S(2)}, u32[]{:S(2)}) collective-permute-start(bf16[144,128]{1,0:T(8,128)(2,1)S(1)} %collective-permute-done.1.far), channel_id=1, source_target_pairs={{0,32},{1,33},{2,34},{3,35},{4,36},{5,37},{6,38},{7,39},{8,40},{9,... | collective-permute-start | bytes 110600 | tf_op jit(solution)/shard_map/ppermute | solution.py:333
  29.1 1.2 %collective-permute-done.2.swapped = bf16[144,128]{1,0:T(8,128)(2,1)S(1)} collective-permute-done((bf16[144,128]{1,0:T(8,128)(2,1)S(1)}, bf16[144,128]{1,0:T(8,128)(2,1)S(1)}, u32[]{:S(2)}, u32[]{:S(2)}) %collective-permute-start.2) | collective-permute-done | bytes 36896 | tf_op jit(solution)/shard_map/ppermute | solution.py:333
  30.3 0.6 copy-done.7
  30.9 1.5 %vertical_edges.1 = bf16[304,128]{1,0:T(8,128)(2,1)} custom-call(s32[3]{0:T(128)} %pad_add_fusion.place, bf16[128,128]{1,0:T(8,128)(2,1)} %bitcast.26, bf16[128,128]{1,0:T(8,128)(2,1)} %bitcast.30, bf16[144,128]{1,0:T(8,128)(2,1)} %copy-done.5, bf16[144,128]{1,0:T(8,128)(2,1)} %copy-done.7), custom_call_target="tpu_custom_call" | custom-call | tf_op jit(solution)/shard_map/vertical_edges/pallas_call | solution.py:334
  32.4 1.9 %collective-permute-start.3 = (bf16[304,128]{1,0:T(8,128)(2,1)}, bf16[304,128]{1,0:T(8,128)(2,1)S(1)}, u32[]{:S(2)}, u32[]{:S(2)}) collective-permute-start(bf16[304,128]{1,0:T(8,128)(2,1)} %vertical_edges.1), channel_id=1, source_target_pairs={{32,64},{33,65},{34,66},{35,67},{36,68},{37,69},{38,70},{39,71},{4... | collective-permute-start | bytes 233480 | tf_op jit(solution)/shard_map/ppermute | solution.py:341
  34.3 4.0 %collective-permute-done.3.vertical = bf16[304,128]{1,0:T(8,128)(2,1)S(1)} collective-permute-done((bf16[304,128]{1,0:T(8,128)(2,1)}, bf16[304,128]{1,0:T(8,128)(2,1)S(1)}, u32[]{:S(2)}, u32[]{:S(2)}) %collective-permute-start.3) | collective-permute-done | bytes 77856 | tf_op jit(solution)/shard_map/ppermute | solution.py:341
  38.4 0.8 copy-done.6
  39.2 0.8 copy-done.8
  39.9 3.2 %window_attention.1 = (bf16[128,128]{1,0:T(8,128)(2,1)}, bf16[512,128]{1,0:T(8,128)(2,1)S(1)}, bf16[8,128]{1,0:T(8,128)(2,1)S(1)}) custom-call(s32[3]{0:T(128)S(1)} %copy-done.12, f32[2]{0:T(128)S(1)} %copy-done.13, bf16[128,128]{1,0:T(8,128)(2,1)S(1)} %bitcast.27, bf16[128,128]{1,0:T(8,128)(2,1)S(1)} %bitcast.31, bf16[128,128]{1,0:T(8,128)(2,1)S(1)} %copy-done.4, ...), custom_call_target="tpu_custom_call" | custom-call | tf_op jit(solution)/shard_map/window_attention/pallas_call | solution.py:347
  43.1 14.7 %all_to_all.15 = bf16[32,24,128]{2,1,0:T(8,128)(2,1)S(1)} all-to-all(bf16[32,24,128]{2,1,0:T(8,128)(2,1)S(1)} %pad_maximum_fusion), channel_id=1, replica_groups=mesh['lo'=8,'core'=2,'x'=4,'y'=4,'hi'=2] {'x','y','core'}, dimensions={0} | all-to-all | bytes 393216 | tf_op jit(solution)/shard_map/all_to_all | solution.py:308
  57.9 0.1 reshape.85
  58.0 0.1 reduce_sum.39
  58.1 0.1 copy.12
  58.2 0.1 reshape.86
  58.3 25.8 %all_to_all.16 = bf16[16,24,128]{2,1,0:T(8,128)(2,1)S(1)} all-to-all(bf16[16,24,128]{2,1,0:T(8,128)(2,1)S(1)} %broadcast_in_dim.7), channel_id=1, replica_groups=mesh['lo'=8,'core'=2,'x'=4,'y'=4,'hi'=2] {'lo','hi'}, dimensions={0} | all-to-all | bytes 196608 | tf_op jit(solution)/shard_map/all_to_all | solution.py:308
  84.1 0.7 broadcast_in_dim.8
  84.8 5.6 %all-to-all-start.2 = ((bf16[32,16,128]{2,1,0:T(8,128)(2,1)}), bf16[32,16,128]{2,1,0:T(8,128)(2,1)S(1)}, u32[]{:S(2)}, u32[]{:S(2)}) async-start(bf16[32,16,128]{2,1,0:T(8,128)(2,1)} %broadcast_in_dim.8), calls=%async_computation.2 | async-start | bytes 262144 | tf_op jit(solution)/shard_map/all_to_all | solution.py:308
  90.5 0.1 reshape_squeeze.3
  90.5 0.6 reduce_sum.42
  91.2 7.1 %all-to-all-done.2 = bf16[32,16,128]{2,1,0:T(8,128)(2,1)S(1)} async-done(((bf16[32,16,128]{2,1,0:T(8,128)(2,1)}), bf16[32,16,128]{2,1,0:T(8,128)(2,1)S(1)}, u32[]{:S(2)}, u32[]{:S(2)}) %all-to-all-start.2) | async-done | bytes 131104 | tf_op jit(solution)/shard_map/all_to_all | solution.py:308
  98.3 0.6 fusion.3
  98.9 0.7 pad_maximum_fusion.1
  (35 shorter events, 0.2 us)
Async XLA Ops:
  0.6 37.7 %copy-start.2 = (f32[2,352,8]{2,1,0:T(8,128)S(1)}, f32[2,352,8]{2,1,0:T(8,128)}, u32[]{:S(2)}) copy-start(f32[2,352,8]{2,1,0:T(8,128)} %constant.37.clone.query_spots) | copy-start | bytes 67588
  1.5 9.7 %collective-permute-start = (bf16[2,128,128]{2,1,0:T(8,128)(2,1)S(1)}, bf16[2,128,128]{2,1,0:T(8,128)(2,1)S(1)}, u32[]{:S(2)}, u32[]{:S(2)}) collective-permute-start(bf16[2,128,128]{2,1,0:T(8,128)(2,1)S(1)} %pad_maximum_fusion.2), channel_id=1, source_target_pairs={{0,32},{1,33},{2,34},{3,35},{4,36},{5,37},{6,38},{7,39},{8,40},{9,... | collective-permute-start | bytes 196616 | tf_op jit(solution)/shard_map/ppermute | solution.py:323
  11.8 26.6 %copy-start.9 = (bf16[128,384]{1,0:T(8,128)(2,1)S(1)}, bf16[128,384]{1,0:T(8,128)(2,1)}, u32[]{:S(2)}) copy-start(bf16[128,384]{1,0:T(8,128)(2,1)} %w_qkv.1) | copy-start | bytes 294916
  13.4 24.9 %copy-start = (bf16[8,16,128]{2,1,0:T(8,128)(2,1)S(1)}, bf16[8,16,128]{2,1,0:T(8,128)(2,1)}, u32[]{:S(2)}) copy-start(bf16[8,16,128]{2,1,0:T(8,128)(2,1)} %param.7) | copy-start | bytes 98308
  13.4 24.9 %copy-start.1 = (bf16[8,16,128]{2,1,0:T(8,128)(2,1)S(1)}, bf16[8,16,128]{2,1,0:T(8,128)(2,1)}, u32[]{:S(2)}) copy-start(bf16[8,16,128]{2,1,0:T(8,128)(2,1)} %param.8) | copy-start | bytes 98308
  13.4 24.9 %copy-start.3 = (bf16[128,128]{1,0:T(8,128)(2,1)S(1)}, bf16[128,128]{1,0:T(8,128)(2,1)}, u32[]{:S(2)}) copy-start(bf16[128,128]{1,0:T(8,128)(2,1)} %get-tuple-element.14.other_cot) | copy-start | bytes 98308
  13.4 24.9 %copy-start.4 = (bf16[128,128]{1,0:T(8,128)(2,1)S(1)}, bf16[128,128]{1,0:T(8,128)(2,1)}, u32[]{:S(2)}) copy-start(bf16[128,128]{1,0:T(8,128)(2,1)} %get-tuple-element.15.other_feat) | copy-start | bytes 98308
  13.4 24.9 %copy-start.10 = (f32[2,8,640]{2,1,0:T(8,128)S(1)}, f32[2,8,640]{2,1,0:T(8,128)}, u32[]{:S(2)}) copy-start(f32[2,8,640]{2,1,0:T(8,128)} %constant.36.clone.key_spots) | copy-start | bytes 122884
  13.4 24.9 %copy-start.11 = (bf16[128,128]{1,0:T(8,128)(2,1)S(1)}, bf16[128,128]{1,0:T(8,128)(2,1)}, u32[]{:S(2)}) copy-start(bf16[128,128]{1,0:T(8,128)(2,1)} %w_out.1) | copy-start | bytes 98308
  13.4 24.9 %copy-start.12 = (s32[3]{0:T(128)S(1)}, s32[3]{0:T(128)}, u32[]{:S(2)}) copy-start(s32[3]{0:T(128)} %pad_add_fusion.place) | copy-start | bytes 40
  13.4 24.9 %copy-start.13 = (f32[2]{0:T(128)S(1)}, f32[2]{0:T(128)}, u32[]{:S(2)}) copy-start(f32[2]{0:T(128)} %cos_scale.1) | copy-start | bytes 28
  13.5 13.8 %collective-permute-start.1 = (bf16[144,128]{1,0:T(8,128)(2,1)}, bf16[144,128]{1,0:T(8,128)(2,1)S(1)}, u32[]{:S(2)}, u32[]{:S(2)}) collective-permute-start(bf16[144,128]{1,0:T(8,128)(2,1)} %far_edges.1), channel_id=1, source_target_pairs={{0,1},{1,2},{2,3},{3,4},{4,5},{5,6},{6,7},{7,8},{8,9},{9,10},{10,1... | collective-permute-start | bytes 110600 | tf_op jit(solution)/shard_map/ppermute | solution.py:332
  27.2 3.1 %copy-start.5 = (bf16[144,128]{1,0:T(8,128)(2,1)}, bf16[144,128]{1,0:T(8,128)(2,1)S(1)}, u32[]{:S(2)}) copy-start(bf16[144,128]{1,0:T(8,128)(2,1)S(1)} %collective-permute-done.1.far) | copy-start | bytes 110596
  27.2 3.1 %collective-permute-start.2 = (bf16[144,128]{1,0:T(8,128)(2,1)S(1)}, bf16[144,128]{1,0:T(8,128)(2,1)S(1)}, u32[]{:S(2)}, u32[]{:S(2)}) collective-permute-start(bf16[144,128]{1,0:T(8,128)(2,1)S(1)} %collective-permute-done.1.far), channel_id=1, source_target_pairs={{0,32},{1,33},{2,34},{3,35},{4,36},{5,37},{6,38},{7,39},{8,40},{9,... | collective-permute-start | bytes 110600 | tf_op jit(solution)/shard_map/ppermute | solution.py:333
  30.3 0.6 copy-start.7
  32.4 5.9 %collective-permute-start.3 = (bf16[304,128]{1,0:T(8,128)(2,1)}, bf16[304,128]{1,0:T(8,128)(2,1)S(1)}, u32[]{:S(2)}, u32[]{:S(2)}) collective-permute-start(bf16[304,128]{1,0:T(8,128)(2,1)} %vertical_edges.1), channel_id=1, source_target_pairs={{32,64},{33,65},{34,66},{35,67},{36,68},{37,69},{38,70},{39,71},{4... | collective-permute-start | bytes 233480 | tf_op jit(solution)/shard_map/ppermute | solution.py:341
  38.4 0.8 copy-start.6
  39.2 0.8 copy-start.8
  84.8 13.4 %all-to-all-start.2 = ((bf16[32,16,128]{2,1,0:T(8,128)(2,1)}), bf16[32,16,128]{2,1,0:T(8,128)(2,1)S(1)}, u32[]{:S(2)}, u32[]{:S(2)}) async-start(bf16[32,16,128]{2,1,0:T(8,128)(2,1)} %broadcast_in_dim.8), calls=%async_computation.2 | async-start | bytes 262144 | tf_op jit(solution)/shard_map/all_to_all | solution.py:308

commit v2 on v1

--- a/solution.py
+++ b/solution.py
@@ -6,7 +6,6 @@
 from jax import lax
 from jax.experimental import pallas as pl
 from jax.experimental.pallas import tpu as pltpu
-from jax.sharding import Mesh
 from jax.sharding import PartitionSpec as P
 
 RADIUS = 3
@@ -15,10 +14,12 @@
 HEAD = 64
 ROWS, COLS = 8, 16
 OWN = ROWS * COLS
-QUERIES = 352
+QUERIES = 368
 KEYS = 640
 NEAR = 384
-BLOCK = 32
+BLOCK = 16
+EDGE = 24
+SENT = 80
 SHARES = 32
 LOG2E = 1.4426950408889634
 FAR_AWAY = 1e4
@@ -38,30 +39,33 @@
         token = start + np.arange(count)
         return np.stack([8 * holder + token // 16 + lift, token % 16])
 
-    def edge(start, count, left, inner, lift):
-        token = start + np.arange(count)
-        return np.stack([token // 3 + lift, token % 3 + side_columns(left, inner)])
+    def edge(holder, left, inner, lift):
+        token = np.arange(EDGE)
+        row = 8 * holder + token // 3 + lift
+        return np.stack([row, token % 3 + side_columns(left, inner)])
 
     other = 1 - core
     lift = -16 if core == 0 else 16
-    far_left = core == 0
-    sent_left = other == 0
+    left = core == 0
     pieces = [
         tile(core, 0, 128, 0),
         tile(other, 80 * core, 48, 0),
-        edge(0, 48, far_left, True, 0),
-        edge(0, 48, not far_left, True, 0),
+        edge(core, left, True, 0),
+        edge(other, left, True, 0),
+        edge(other, not left, True, 0),
+        edge(core, not left, True, 0),
         tile(other, 80 * other, 48, lift),
-        edge(32 * other, 16, sent_left, True, lift),
-        edge(32 * other, 16, not sent_left, True, lift),
+        edge(other, not left, True, lift),
+        edge(other, left, True, lift),
         tile(other, 48 - 16 * core, 48, 0),
-        edge(0, 48, far_left, False, 0),
-        edge(0, 48, not far_left, False, 0),
+        edge(core, left, False, 0),
+        edge(other, left, False, 0),
+        edge(other, not left, False, 0),
+        edge(core, not left, False, 0),
         tile(other, 48 - 16 * other, 48, lift),
-        edge(16, 16, sent_left, True, lift),
-        edge(16 * other, 32, sent_left, False, lift),
-        edge(16, 16, not sent_left, True, lift),
-        edge(16 * other, 32, not sent_left, False, lift),
+        edge(other, not left, False, lift),
+        edge(other, left, False, lift),
+        np.full((2, 32), FAR_AWAY),
     ]
     return np.concatenate(pieces, axis=1).astype(np.float32)
 
@@ -89,42 +93,33 @@
     return jnp.dot(left, right, preferred_element_type=F32)
 
 
-def far_kernel(place, feat, cot, other_feat, other_cot, out):
+def edge_kernel(place, feat, cot, own_edge, mate_edge, tile):
     core = place[0]
-    spot = lax.broadcasted_iota(jnp.int32, (96, 128), 0)
-    token = lax.broadcasted_iota(jnp.int32, (96, 128), 1)
-    outer = jnp.where(spot >= 48, 1, 0)
-    index = spot - 48 * outer
+    spot = lax.broadcasted_iota(jnp.int32, (SENT, 128), 0)
+    token = lax.broadcasted_iota(jnp.int32, (SENT, 128), 1)
+    kind = jnp.where(spot >= EDGE, 1, 0) + jnp.where(spot >= 2 * EDGE, 1, 0)
+    index = spot - EDGE * kind
     row = (index * 43) >> 7
     step = index - 3 * row
-    column = step + jnp.where(core == 0, 13 - 3 * outer, 3 * outer)
-    half = row >> 3
-    wanted = (row - 8 * half) * 16 + column
-    mine = jnp.where((wanted == token) & (half == core), 1.0, 0.0).astype(BF16)
-    theirs = jnp.where((wanted == token) & (half != core), 1.0, 0.0).astype(BF16)
-    out[0:96, :] = (dot_nn(mine, feat[...]) + dot_nn(theirs, other_feat[...])).astype(BF16)
-    out[96:144, :] = (
-        dot_nn(mine[0:48], cot[...]) + dot_nn(theirs[0:48], other_cot[...])
-    ).astype(BF16)
+    outer = kind == 1
+    right = row * 16 + step + jnp.where(outer, 10, 13)
+    left = row * 16 + step + jnp.where(outer, 3, 0)
+    used = spot < 3 * EDGE
+    from_cot = kind == 2
+    for ref, wanted in (
+        (own_edge, jnp.where(core == 0, right, left)),
+        (mate_edge, jnp.where(core == 0, left, right)),
+    ):
+        hit = (wanted == token) & used
+        of_feat = jnp.where(hit & ~from_cot, 1.0, 0.0).astype(BF16)
+        of_cot = jnp.where(hit & from_cot, 1.0, 0.0).astype(BF16)
+        ref[...] = (dot_nn(of_feat, feat[...]) + dot_nn(of_cot, cot[...])).astype(BF16)
+    tile[0:OWN, :] = feat[...]
+    tile[OWN:, :] = cot[...]
 
 
 def rows_at(ref, start, count):
     return ref[pl.ds(pl.multiple_of(start, 16), count), :]
-
-
-def vertical_kernel(place, feat, cot, far, swapped, out):
-    core = place[0]
-    out[0:48, :] = rows_at(feat, 80 * core, 48)
-    out[48:64, :] = rows_at(far, 32 * core, 16)
-    out[64:80, :] = rows_at(swapped, 32 * core, 16)
-    out[80:128, :] = rows_at(feat, 48 - 16 * core, 48)
-    out[128:144, :] = far[16:32, :]
-    out[144:176, :] = rows_at(far, 48 + 16 * core, 32)
-    out[176:192, :] = swapped[16:32, :]
-    out[192:224, :] = rows_at(swapped, 48 + 16 * core, 32)
-    out[224:272, :] = rows_at(cot, 80 * core, 48)
-    out[272:288, :] = rows_at(far, 96 + 32 * core, 16)
-    out[288:304, :] = rows_at(swapped, 96 + 32 * core, 16)
 
 
 def attention_kernel(
@@ -132,11 +127,12 @@
     cos_scale,
     feat,
     cot,
-    other_feat,
-    other_cot,
+    mate,
+    next_chip,
     far,
-    swapped,
-    vertical,
+    far_mate,
+    far_next,
+    far_skip,
     w_qkv,
     w_out,
     key_spots,
@@ -159,20 +155,39 @@
     slope_key,
 ):
     core = place[0]
+    other = 1 - core
+    far_wide = far[...].astype(F32)
+    mate_wide = far_mate[...].astype(F32)
+    next_wide = far_next[0:SENT, :].astype(F32)
+    skip_wide = far_skip[SENT:, :].astype(F32)
+    edges = (
+        far_wide[:SENT],
+        far_wide[SENT:],
+        mate_wide[:SENT],
+        mate_wide[SENT:],
+        next_wide,
+        skip_wide,
+    )
+
+    def strip(kind, chosen):
+        pieces = [edge[kind * EDGE : (kind + 1) * EDGE] for edge in chosen]
+        return jnp.concatenate(pieces, axis=0).astype(BF16)
+
     tokens[0:128, :] = feat[...]
-    tokens[128:176, :] = rows_at(other_feat, 80 * core, 48)
-    tokens[176:224, :] = far[0:48, :]
-    tokens[224:272, :] = swapped[0:48, :]
-    tokens[272:352, :] = vertical[0:80, :]
-    tokens[352:400, :] = rows_at(other_feat, 48 - 16 * core, 48)
-    tokens[400:448, :] = far[48:96, :]
-    tokens[448:496, :] = swapped[48:96, :]
-    tokens[496:640, :] = vertical[80:224, :]
+    tokens[128:176, :] = rows_at(mate, 80 * core, 48)
+    tokens[176:272, :] = strip(0, edges[:4])
+    tokens[272:320, :] = rows_at(next_chip, 80 * other, 48)
+    tokens[320:368, :] = strip(0, edges[4:])
+    tokens[368:416, :] = rows_at(mate, 48 - 16 * core, 48)
+    tokens[416:512, :] = strip(1, edges[:4])
+    tokens[512:560, :] = rows_at(next_chip, 48 - 16 * other, 48)
+    tokens[560:608, :] = strip(1, edges[4:])
+    tokens[608:640, :] = jnp.zeros((32, MODEL), BF16)
     cots[0:128, :] = cot[...]
-    cots[128:176, :] = rows_at(other_cot, 80 * core, 48)
-    cots[176:224, :] = far[96:144, :]
-    cots[224:272, :] = swapped[96:144, :]
-    cots[272:352, :] = vertical[224:304, :]
+    cots[128:176, :] = rows_at(mate, OWN + 80 * core, 48)
+    cots[176:272, :] = strip(2, edges[:4])
+    cots[272:320, :] = rows_at(next_chip, OWN + 80 * other, 48)
+    cots[320:368, :] = strip(2, edges[4:])
 
     keys[...] = dot_nn(tokens[...], w_qkv[:, MODEL : 2 * MODEL]).astype(BF16)
     values[...] = dot_nn(tokens[...], w_qkv[:, 2 * MODEL :]).astype(BF16)
@@ -296,49 +311,65 @@
     return found
 
 
-EVERY = ("lo", "core", "x", "y", "hi")
-PLANE = ("x", "y", "core")
-LINE = ("lo", "hi")
+EVERY = ("row", "col")
+
+
+def device(x, y, z, core):
+    return ((z % 8) * 2 + core) * 32 + (x % 4) * 8 + (y % 4) * 2 + z // 8 % 2
+
+
+FIRST_X, FIRST_Y, FIRST_Z = 2, 2, 8
+PLANES = [
+    [
+        device(x + FIRST_X, y + FIRST_Y, z, core)
+        for x in range(4)
+        for y in range(4)
+        for core in range(2)
+    ]
+    for z in range(16)
+]
+LINES = [
+    [device(x, y, z + FIRST_Z, core) for z in range(16)]
+    for x in range(4)
+    for y in range(4)
+    for core in range(2)
+]
 CHIP_MATE = pairs(lambda row, col: (row ^ 1, col))
 FAR_MATE = pairs(lambda row, col: (row, col - 1 if row % 2 else col + 1))
 NEXT_CHIP = pairs(lambda row, col: (row + 1 if row % 2 else row - 1, col))
-
-
-def exchange(array, axes):
-    return lax.all_to_all(array, axes, 0, 0, tiled=True)
-
-
-def to_all(array, axes, count):
-    return exchange(jnp.broadcast_to(array[None], (count,) + array.shape), axes)
+SKIP_CHIP = pairs(lambda row, col: (row - 2 if row % 2 else row + 2, col))
+
+
+def exchange(array, groups):
+    return lax.all_to_all(array, EVERY, 0, 0, axis_index_groups=groups, tiled=True)
+
+
+def to_all(array, groups):
+    return exchange(jnp.broadcast_to(array[None], (len(groups[0]),) + array.shape), groups)
 
 
 def on_device(features, cotangent, w_qkv, w_out, cos_scale):
-    core = lax.axis_index("core")
-    col = lax.axis_index(("x", "y", "hi"))
-    place = jnp.stack([core, lax.axis_index("lo") * 16, col * 16]).astype(jnp.int32)
+    row, col = lax.axis_index("row"), lax.axis_index("col")
+    place = jnp.stack([row % 2, row // 2 * 16, col * 16]).astype(jnp.int32)
     feat = features.reshape(OWN, MODEL)
     cot = cotangent.reshape(OWN, MODEL)
     smem = pl.BlockSpec(memory_space=pltpu.SMEM)
 
-    other = lax.ppermute(jnp.stack([feat, cot]), EVERY, CHIP_MATE)
-    other_feat, other_cot = other[0], other[1]
-    far_out = pl.pallas_call(
-        far_kernel,
-        out_shape=jax.ShapeDtypeStruct((144, MODEL), BF16),
-        in_specs=[smem] + vmem(4),
-        out_specs=vmem(1)[0],
-        name="far_edges",
-    )(place, feat, cot, other_feat, other_cot)
-    far = lax.ppermute(far_out, EVERY, FAR_MATE)
-    swapped = lax.ppermute(far, EVERY, CHIP_MATE)
-    vertical_out = pl.pallas_call(
-        vertical_kernel,
-        out_shape=jax.ShapeDtypeStruct((304, MODEL), BF16),
-        in_specs=[smem] + vmem(4),
-        out_specs=vmem(1)[0],
-        name="vertical_edges",
-    )(place, feat, cot, far, swapped)
-    vertical = lax.ppermute(vertical_out, EVERY, NEXT_CHIP)
+    edge = jax.ShapeDtypeStruct((SENT, MODEL), BF16)
+    own_edge, mate_edge, tile = pl.pallas_call(
+        edge_kernel,
+        out_shape=(edge, edge, jax.ShapeDtypeStruct((2 * OWN, MODEL), BF16)),
+        in_specs=[smem] + vmem(2),
+        out_specs=vmem(3),
+        name="edges",
+    )(place, feat, cot)
+    other_edge = lax.ppermute(mate_edge, EVERY, CHIP_MATE)
+    far = lax.ppermute(jnp.concatenate([own_edge, other_edge]), EVERY, FAR_MATE)
+    mate = lax.ppermute(tile, EVERY, CHIP_MATE)
+    next_chip = lax.ppermute(tile, EVERY, NEXT_CHIP)
+    far_mate = lax.ppermute(far, EVERY, CHIP_MATE)
+    far_next = lax.ppermute(far, EVERY, NEXT_CHIP)
+    far_skip = lax.ppermute(far, EVERY, SKIP_CHIP)
 
     key_spots = np.zeros((2, 8, KEYS), np.float32)
     key_spots[:, :2] = TABLES
@@ -351,7 +382,7 @@
             jax.ShapeDtypeStruct((4 * MODEL, MODEL), BF16),
             jax.ShapeDtypeStruct((8, MODEL), BF16),
         ),
-        in_specs=[smem, smem] + vmem(11),
+        in_specs=[smem, smem] + vmem(12),
         out_specs=vmem(3),
         scratch_shapes=[
             pltpu.VMEM((KEYS, MODEL), BF16),
@@ -375,11 +406,12 @@
         cos_scale,
         feat,
         cot,
-        other_feat,
-        other_cot,
+        mate,
+        next_chip,
         far,
-        swapped,
-        vertical,
+        far_mate,
+        far_next,
+        far_skip,
         w_qkv,
         w_out,
         jnp.asarray(key_spots),
@@ -388,7 +420,7 @@
 
     scale_rows = jnp.broadcast_to(scale_tile[None], (SHARES, 8, MODEL))
     shares = jnp.concatenate([grad_w.reshape(SHARES, 16, MODEL), scale_rows], axis=1)
-    share = jnp.sum(exchange(shares, PLANE).astype(F32), axis=0)
+    share = jnp.sum(exchange(shares, PLANES).astype(F32), axis=0)
     pieces = share[16:17, 0:6].reshape(2, 3)
     scale_part = jnp.sum(pieces, axis=1, keepdims=True)
     top = lax.reduce_precision(scale_part, 8, 7)
@@ -396,20 +428,19 @@
     split = jnp.concatenate([top, middle, scale_part - top - middle], axis=1)
     split = jnp.pad(split.reshape(1, 6), ((0, 7), (0, MODEL - 6)))
     share = jnp.concatenate([share[:16], split], axis=0).astype(BF16)
-    share = jnp.sum(to_all(share, LINE, 16).astype(F32), axis=0)
+    share = jnp.sum(to_all(share, LINES).astype(F32), axis=0)
     grad_scale = jnp.sum(share[16, 0:6].reshape(2, 3), axis=1)
-    whole = to_all(share[:16].astype(BF16), PLANE, SHARES).astype(F32)
+    whole = to_all(share[:16].astype(BF16), PLANES).astype(F32)
     whole = whole.reshape(4, MODEL, MODEL)
     grad_w_qkv = jnp.concatenate([whole[0], whole[1], whole[2]], axis=1)
     return (grad_feat.reshape(ROWS, COLS, MODEL), grad_w_qkv, whole[3], grad_scale)
 
 
 def solution(mesh):
-    fine = Mesh(mesh.devices.reshape(8, 2, 4, 4, 2), EVERY)
-    tokens = P(("lo", "core"), ("x", "y", "hi"), None)
+    tokens = P("row", "col", None)
     return jax.shard_map(
         on_device,
-        mesh=fine,
+        mesh=mesh,
         in_specs=(tokens, tokens, P(), P(), P()),
         out_specs=(tokens, P(), P(), P()),
         check_vma=False,

time: 100 us -> 90.4 us (0.904)
  starting transfers between devices: 19.6 us -> 41.5 us
  waiting for transfers between devices: 24.8 us -> 4.18 us
  blocking collectives: 40.4 us -> 31.3 us
  Pallas kernels: 6.27 us -> 4.8 us
    ppermute x4 -> x7, starting transfers between devices: 14 us -> 31.8 us  [the longest x1 11.9 us: on_device(): next_chip = lax.ppermute(tile, EVERY, NEXT_CHIP)]
    ppermute x4 -> x7, waiting for transfers between devices: 17.7 us -> 2.19 us  [the longest x1 1.14 us: on_device(): far_mate = lax.ppermute(far, EVERY, CHIP_MATE)]
    all_to_all x2, blocking collectives: 40.4 us -> 31.3 us  [exchange(): lax.all_to_all(array, EVERY, 0, 0, axis_index_groups=groups, tiled=True)]
    all_to_all x1, waiting for transfers between devices: 7.08 us -> 1.99 us  [exchange(): lax.all_to_all(array, EVERY, 0, 0, axis_index_groups=groups, tiled=True)]
    all_to_all x1, starting transfers between devices: 5.62 us -> 9.72 us  [exchange(): lax.all_to_all(array, EVERY, 0, 0, axis_index_groups=groups, tiled=True)]
    pallas_call x2 -> x1, Pallas kernels: 3.11 us -> 1.61 us  [on_device(): pl.pallas_call(edge_kernel, out_shape=(edge, edge, jax.ShapeDtypeStruct((...]
    unnamed x28 -> x16, local copies, waits for them, and re-layouts: 2.19 us -> 2.4 us
  transfers between devices with their start and end apart: 5 -> 8, of which waited for: 5 -> 3; matrix products, arithmetic and copies ran while one was open for 1% -> 1% of each run, Pallas kernels for 0% -> 0%
where the time goes in v2:
time: 90.4 us; the launch traced here: 89.7 us
  starting transfers between devices  41.5 us (46%)
  blocking collectives  31.3 us (35%)
  Pallas kernels  4.8 us (5%)
  waiting for transfers between devices  4.18 us (5%)
  local copies, waits for them, and re-layouts  4.16 us (5%)
  other arithmetic  2.91 us (3%)
    all_to_all x2, blocking collectives, exchange(): lax.all_to_all(array, EVERY, 0, 0, axis_index_groups=groups, tiled=True)  31.3 us
    ppermute x1, starting transfers between devices, on_device(): next_chip = lax.ppermute(tile, EVERY, NEXT_CHIP)  11.9 us
    all_to_all x1, starting transfers between devices, exchange(): lax.all_to_all(array, EVERY, 0, 0, axis_index_groups=groups, tiled=True)  9.72 us
    ppermute x1, starting transfers between devices, on_device(): other_edge = lax.ppermute(mate_edge, EVERY, CHIP_MATE)  8.77 us
    ppermute x1, starting transfers between devices, on_device(): far_next = lax.ppermute(far, EVERY, NEXT_CHIP)  4.67 us
    pallas_call x1, Pallas kernels, on_device(): pl.pallas_call(attention_kernel, out_shape=(jax.ShapeDtypeStruct((OWN, MO...  3.19 us
    unnamed x16, local copies, waits for them, and re-layouts  2.4 us
    all_to_all x1, waiting for transfers between devices, exchange(): lax.all_to_all(array, EVERY, 0, 0, axis_index_groups=groups, tiled=True)  1.99 us
  transfers between devices with their start and end apart: 8, of which 3 were waited for; matrix products, arithmetic and copies ran while one was open for 1% of the time, Pallas kernels for 0%

profile of v2, /device:TPU:1, one launch (start us, length us, event | category | flops | bytes accessed | tf_op | source)
XLA Modules:
  0.0 89.7 jit_solution(12046225220596687673)
XLA Ops:
  0.6 0.0 copy-start.4
  0.7 0.6 pad_add_fusion.place
  1.3 1.6 %edges.1 = (bf16[80,128]{1,0:T(8,128)(2,1)}, bf16[80,128]{1,0:T(8,128)(2,1)}, bf16[256,128]{1,0:T(8,128)(2,1)}) custom-call(s32[3]{0:T(128)} %pad_add_fusion.place, bf16[128,128]{1,0:T(8,128)(2,1)} %bitcast.19, bf16[128,128]{1,0:T(8,128)(2,1)} %bitcast.21), custom_call_target="tpu_custom_call" | custom-call | tf_op jit(solution)/shard_map/edges/pallas_call | solution.py:359
  2.9 8.8 %collective-permute-start.2 = (bf16[80,128]{1,0:T(8,128)(2,1)}, bf16[80,128]{1,0:T(8,128)(2,1)S(1)}, u32[]{:S(2)}, u32[]{:S(2)}) collective-permute-start(bf16[80,128]{1,0:T(8,128)(2,1)} %get-tuple-element.12), channel_id=1, source_target_pairs={{0,32},{1,33},{2,34},{3,35},{4,36},{5,37},{6,38},{7,39},{8,40},{9,... | collective-permute-start | bytes 61448 | tf_op jit(solution)/shard_map/ppermute | solution.py:366
  11.7 1.0 %collective-permute-done.2 = bf16[80,128]{1,0:T(8,128)(2,1)S(1)} collective-permute-done((bf16[80,128]{1,0:T(8,128)(2,1)}, bf16[80,128]{1,0:T(8,128)(2,1)S(1)}, u32[]{:S(2)}, u32[]{:S(2)}) %collective-permute-start.2) | collective-permute-done | bytes 20512 | tf_op jit(solution)/shard_map/ppermute | solution.py:366
  12.7 0.7 pad_maximum_fusion.2
  13.5 1.3 %collective-permute-start.3 = (bf16[160,128]{1,0:T(8,128)(2,1)S(1)}, bf16[160,128]{1,0:T(8,128)(2,1)S(1)}, u32[]{:S(2)}, u32[]{:S(2)}) collective-permute-start(bf16[160,128]{1,0:T(8,128)(2,1)S(1)} %pad_maximum_fusion.2), channel_id=1, source_target_pairs={{0,1},{1,2},{2,3},{3,4},{4,5},{5,6},{6,7},{7,8},{8,9},{9,10},{10,1... | collective-permute-start | bytes 122888 | tf_op jit(solution)/shard_map/ppermute | solution.py:367
  14.8 11.9 %collective-permute-start.1 = (bf16[256,128]{1,0:T(8,128)(2,1)}, bf16[256,128]{1,0:T(8,128)(2,1)S(1)}, u32[]{:S(2)}, u32[]{:S(2)}) collective-permute-start(bf16[256,128]{1,0:T(8,128)(2,1)} %get-tuple-element.10), channel_id=1, source_target_pairs={{32,64},{33,65},{34,66},{35,67},{36,68},{37,69},{38,70},{39,71},{4... | collective-permute-start | bytes 196616 | tf_op jit(solution)/shard_map/ppermute | solution.py:369
  26.7 1.9 %collective-permute-start = (bf16[256,128]{1,0:T(8,128)(2,1)}, bf16[256,128]{1,0:T(8,128)(2,1)S(1)}, u32[]{:S(2)}, u32[]{:S(2)}) collective-permute-start(bf16[256,128]{1,0:T(8,128)(2,1)} %get-tuple-element.10), channel_id=1, source_target_pairs={{0,32},{1,33},{2,34},{3,35},{4,36},{5,37},{6,38},{7,39},{8,40},{9,... | collective-permute-start | bytes 196616 | tf_op jit(solution)/shard_map/ppermute | solution.py:368
  28.6 0.0 collective-permute-done.3.far
  28.6 1.3 %collective-permute-start.6 = (bf16[160,128]{1,0:T(8,128)(2,1)S(1)}, bf16[160,128]{1,0:T(8,128)(2,1)S(1)}, u32[]{:S(2)}, u32[]{:S(2)}) collective-permute-start(bf16[160,128]{1,0:T(8,128)(2,1)S(1)} %collective-permute-done.3.far), channel_id=1, source_target_pairs={{0,64},{1,65},{2,66},{3,67},{4,68},{5,69},{6,70},{7,71},{8,72},{9,... | collective-permute-start | bytes 122888 | tf_op jit(solution)/shard_map/ppermute | solution.py:372
  29.9 4.7 %collective-permute-start.5 = (bf16[160,128]{1,0:T(8,128)(2,1)S(1)}, bf16[160,128]{1,0:T(8,128)(2,1)S(1)}, u32[]{:S(2)}, u32[]{:S(2)}) collective-permute-start(bf16[160,128]{1,0:T(8,128)(2,1)S(1)} %collective-permute-done.3.far), channel_id=1, source_target_pairs={{32,64},{33,65},{34,66},{35,67},{36,68},{37,69},{38,70},{39,71},{4... | collective-permute-start | bytes 122888 | tf_op jit(solution)/shard_map/ppermute | solution.py:371
  34.6 1.9 %collective-permute-start.4 = (bf16[160,128]{1,0:T(8,128)(2,1)S(1)}, bf16[160,128]{1,0:T(8,128)(2,1)S(1)}, u32[]{:S(2)}, u32[]{:S(2)}) collective-permute-start(bf16[160,128]{1,0:T(8,128)(2,1)S(1)} %collective-permute-done.3.far), channel_id=1, source_target_pairs={{0,32},{1,33},{2,34},{3,35},{4,36},{5,37},{6,38},{7,39},{8,40},{9,... | collective-permute-start | bytes 122888 | tf_op jit(solution)/shard_map/ppermute | solution.py:370
  36.6 1.1 %collective-permute-done.4.far_mate = bf16[160,128]{1,0:T(8,128)(2,1)S(1)} collective-permute-done((bf16[160,128]{1,0:T(8,128)(2,1)S(1)}, bf16[160,128]{1,0:T(8,128)(2,1)S(1)}, u32[]{:S(2)}, u32[]{:S(2)}) %collective-permute-start.4) | collective-permute-done | bytes 40992 | tf_op jit(solution)/shard_map/ppermute | solution.py:370
  37.8 0.0 copy-start
  37.8 1.0 %copy-done = f32[2,368,8]{2,1,0:T(8,128)S(1)} copy-done((f32[2,368,8]{2,1,0:T(8,128)S(1)}, f32[2,368,8]{2,1,0:T(8,128)}, u32[]{:S(2)}) %copy-start) | copy-done | bytes 23576
  38.8 0.8 copy-done.5
  39.5 0.6 copy-done.6
  40.1 3.2 %window_attention.1 = (bf16[128,128]{1,0:T(8,128)(2,1)}, bf16[512,128]{1,0:T(8,128)(2,1)S(1)}, bf16[8,128]{1,0:T(8,128)(2,1)S(1)}) custom-call(s32[3]{0:T(128)S(1)} %copy-done.6, f32[2]{0:T(128)S(1)} %copy-done.7, bf16[128,128]{1,0:T(8,128)(2,1)S(1)} %bitcast.20, bf16[128,128]{1,0:T(8,128)(2,1)S(1)} %bitcast.22, ...), custom_call_target="tpu_custom_call" | custom-call | tf_op jit(solution)/shard_map/window_attention/pallas_call | solution.py:378
  43.4 13.2 %all_to_all.15 = bf16[32,24,128]{2,1,0:T(8,128)(2,1)S(1)} all-to-all(bf16[32,24,128]{2,1,0:T(8,128)(2,1)S(1)} %pad_maximum_fusion), channel_id=1, replica_groups={{20,52,22,54,16,48,18,50,28,60,30,62,24,56,26,58,4,36,6,38,0,32,2,34,12..., dimensions={0} | all-to-all | bytes 393216 | tf_op jit(solution)/shard_map/all_to_all | solution.py:344
  56.7 0.1 reshape.85
  56.7 0.1 reduce_sum.39
  56.9 0.1 copy.12
  57.0 0.1 reshape.86
  57.1 18.1 %all_to_all.16 = bf16[16,24,128]{2,1,0:T(8,128)(2,1)S(1)} all-to-all(bf16[16,24,128]{2,1,0:T(8,128)(2,1)S(1)} %broadcast_in_dim.7), channel_id=1, replica_groups={{1,65,129,193,257,321,385,449,0,64,128,192,256,320,384,448},{33,97,161,..., dimensions={0} | all-to-all | bytes 196608 | tf_op jit(solution)/shard_map/all_to_all | solution.py:344
  75.3 0.7 broadcast_in_dim.8
  75.9 9.7 %all-to-all-start.2 = ((bf16[32,16,128]{2,1,0:T(8,128)(2,1)}), bf16[32,16,128]{2,1,0:T(8,128)(2,1)S(1)}, u32[]{:S(2)}, u32[]{:S(2)}) async-start(bf16[32,16,128]{2,1,0:T(8,128)(2,1)} %broadcast_in_dim.8), calls=%async_computation.2 | async-start | bytes 262144 | tf_op jit(solution)/shard_map/all_to_all | solution.py:344
  85.7 0.1 reshape_squeeze.3
  85.8 0.6 reduce_sum.42
  86.4 2.0 %all-to-all-done.2 = bf16[32,16,128]{2,1,0:T(8,128)(2,1)S(1)} async-done(((bf16[32,16,128]{2,1,0:T(8,128)(2,1)}), bf16[32,16,128]{2,1,0:T(8,128)(2,1)S(1)}, u32[]{:S(2)}, u32[]{:S(2)}) %all-to-all-start.2) | async-done | bytes 131104 | tf_op jit(solution)/shard_map/all_to_all | solution.py:344
  88.4 0.6 fusion.3
  89.0 0.7 pad_maximum_fusion.1
  (27 shorter events, 0.2 us)
Async XLA Ops:
  0.6 37.1 %copy-start.7 = (f32[2]{0:T(128)S(1)}, f32[2]{0:T(128)}, u32[]{:S(2)}) copy-start(f32[2]{0:T(128)} %cos_scale.1) | copy-start | bytes 28
  0.6 37.1 %copy-start.4 = (f32[2,8,640]{2,1,0:T(8,128)S(1)}, f32[2,8,640]{2,1,0:T(8,128)}, u32[]{:S(2)}) copy-start(f32[2,8,640]{2,1,0:T(8,128)} %constant.45.clone.key_spots) | copy-start | bytes 122884
  0.7 37.1 %copy-start.3 = (bf16[128,384]{1,0:T(8,128)(2,1)S(1)}, bf16[128,384]{1,0:T(8,128)(2,1)}, u32[]{:S(2)}) copy-start(bf16[128,384]{1,0:T(8,128)(2,1)} %w_qkv.1) | copy-start | bytes 294916
  2.9 9.8 %collective-permute-start.2 = (bf16[80,128]{1,0:T(8,128)(2,1)}, bf16[80,128]{1,0:T(8,128)(2,1)S(1)}, u32[]{:S(2)}, u32[]{:S(2)}) collective-permute-start(bf16[80,128]{1,0:T(8,128)(2,1)} %get-tuple-element.12), channel_id=1, source_target_pairs={{0,32},{1,33},{2,34},{3,35},{4,36},{5,37},{6,38},{7,39},{8,40},{9,... | collective-permute-start | bytes 61448 | tf_op jit(solution)/shard_map/ppermute | solution.py:366
  12.7 25.0 %copy-start.1 = (bf16[8,16,128]{2,1,0:T(8,128)(2,1)S(1)}, bf16[8,16,128]{2,1,0:T(8,128)(2,1)}, u32[]{:S(2)}) copy-start(bf16[8,16,128]{2,1,0:T(8,128)(2,1)} %param.7) | copy-start | bytes 98308
  12.7 25.0 %copy-start.2 = (bf16[8,16,128]{2,1,0:T(8,128)(2,1)S(1)}, bf16[8,16,128]{2,1,0:T(8,128)(2,1)}, u32[]{:S(2)}) copy-start(bf16[8,16,128]{2,1,0:T(8,128)(2,1)} %param.8) | copy-start | bytes 98308
  13.5 15.2 %collective-permute-start.3 = (bf16[160,128]{1,0:T(8,128)(2,1)S(1)}, bf16[160,128]{1,0:T(8,128)(2,1)S(1)}, u32[]{:S(2)}, u32[]{:S(2)}) collective-permute-start(bf16[160,128]{1,0:T(8,128)(2,1)S(1)} %pad_maximum_fusion.2), channel_id=1, source_target_pairs={{0,1},{1,2},{2,3},{3,4},{4,5},{5,6},{6,7},{7,8},{8,9},{9,10},{10,1... | collective-permute-start | bytes 122888 | tf_op jit(solution)/shard_map/ppermute | solution.py:367
  14.8 21.8 %collective-permute-start.1 = (bf16[256,128]{1,0:T(8,128)(2,1)}, bf16[256,128]{1,0:T(8,128)(2,1)S(1)}, u32[]{:S(2)}, u32[]{:S(2)}) collective-permute-start(bf16[256,128]{1,0:T(8,128)(2,1)} %get-tuple-element.10), channel_id=1, source_target_pairs={{32,64},{33,65},{34,66},{35,67},{36,68},{37,69},{38,70},{39,71},{4... | collective-permute-start | bytes 196616 | tf_op jit(solution)/shard_map/ppermute | solution.py:369
  26.7 9.9 %collective-permute-start = (bf16[256,128]{1,0:T(8,128)(2,1)}, bf16[256,128]{1,0:T(8,128)(2,1)S(1)}, u32[]{:S(2)}, u32[]{:S(2)}) collective-permute-start(bf16[256,128]{1,0:T(8,128)(2,1)} %get-tuple-element.10), channel_id=1, source_target_pairs={{0,32},{1,33},{2,34},{3,35},{4,36},{5,37},{6,38},{7,39},{8,40},{9,... | collective-permute-start | bytes 196616 | tf_op jit(solution)/shard_map/ppermute | solution.py:368
  28.6 7.9 %collective-permute-start.6 = (bf16[160,128]{1,0:T(8,128)(2,1)S(1)}, bf16[160,128]{1,0:T(8,128)(2,1)S(1)}, u32[]{:S(2)}, u32[]{:S(2)}) collective-permute-start(bf16[160,128]{1,0:T(8,128)(2,1)S(1)} %collective-permute-done.3.far), channel_id=1, source_target_pairs={{0,64},{1,65},{2,66},{3,67},{4,68},{5,69},{6,70},{7,71},{8,72},{9,... | collective-permute-start | bytes 122888 | tf_op jit(solution)/shard_map/ppermute | solution.py:372
  29.9 6.6 %collective-permute-start.5 = (bf16[160,128]{1,0:T(8,128)(2,1)S(1)}, bf16[160,128]{1,0:T(8,128)(2,1)S(1)}, u32[]{:S(2)}, u32[]{:S(2)}) collective-permute-start(bf16[160,128]{1,0:T(8,128)(2,1)S(1)} %collective-permute-done.3.far), channel_id=1, source_target_pairs={{32,64},{33,65},{34,66},{35,67},{36,68},{37,69},{38,70},{39,71},{4... | collective-permute-start | bytes 122888 | tf_op jit(solution)/shard_map/ppermute | solution.py:371
  34.6 3.1 %collective-permute-start.4 = (bf16[160,128]{1,0:T(8,128)(2,1)S(1)}, bf16[160,128]{1,0:T(8,128)(2,1)S(1)}, u32[]{:S(2)}, u32[]{:S(2)}) collective-permute-start(bf16[160,128]{1,0:T(8,128)(2,1)S(1)} %collective-permute-done.3.far), channel_id=1, source_target_pairs={{0,32},{1,33},{2,34},{3,35},{4,36},{5,37},{6,38},{7,39},{8,40},{9,... | collective-permute-start | bytes 122888 | tf_op jit(solution)/shard_map/ppermute | solution.py:370
  37.8 1.0 %copy-start = (f32[2,368,8]{2,1,0:T(8,128)S(1)}, f32[2,368,8]{2,1,0:T(8,128)}, u32[]{:S(2)}) copy-start(f32[2,368,8]{2,1,0:T(8,128)} %constant.46.clone.query_spots) | copy-start | bytes 70660
  38.8 0.8 copy-start.5
  39.5 0.6 copy-start.6
  75.9 12.5 %all-to-all-start.2 = ((bf16[32,16,128]{2,1,0:T(8,128)(2,1)}), bf16[32,16,128]{2,1,0:T(8,128)(2,1)S(1)}, u32[]{:S(2)}, u32[]{:S(2)}) async-start(bf16[32,16,128]{2,1,0:T(8,128)(2,1)} %broadcast_in_dim.8), calls=%async_computation.2 | async-start | bytes 262144 | tf_op jit(solution)/shard_map/all_to_all | solution.py:344

commit v3 on v2

--- a/solution.py
+++ b/solution.py
@@ -93,8 +93,8 @@
     return jnp.dot(left, right, preferred_element_type=F32)
 
 
-def edge_kernel(place, feat, cot, own_edge, mate_edge, tile):
-    core = place[0]
+def edge_kernel(tile, own_edge, mate_edge):
+    core, _, _ = place_here()
     spot = lax.broadcasted_iota(jnp.int32, (SENT, 128), 0)
     token = lax.broadcasted_iota(jnp.int32, (SENT, 128), 1)
     kind = jnp.where(spot >= EDGE, 1, 0) + jnp.where(spot >= 2 * EDGE, 1, 0)
@@ -113,30 +113,60 @@
         hit = (wanted == token) & used
         of_feat = jnp.where(hit & ~from_cot, 1.0, 0.0).astype(BF16)
         of_cot = jnp.where(hit & from_cot, 1.0, 0.0).astype(BF16)
-        ref[...] = (dot_nn(of_feat, feat[...]) + dot_nn(of_cot, cot[...])).astype(BF16)
-    tile[0:OWN, :] = feat[...]
-    tile[OWN:, :] = cot[...]
+        ref[...] = (
+            dot_nn(of_feat, tile[0:OWN, :]) + dot_nn(of_cot, tile[OWN:, :])
+        ).astype(BF16)
+
+
+def place_here():
+    row, col = lax.axis_index("row"), lax.axis_index("col")
+    return row & 1, (row >> 1) * 16, col * 16
 
 
 def rows_at(ref, start, count):
     return ref[pl.ds(pl.multiple_of(start, 16), count), :]
 
 
+def prepare_kernel(
+    cos_scale, tile, _, w_qkv, w_out, key_spots, tile_copy, weights, bias, scales
+):
+    tile_copy[...] = tile[...]
+    head = lax.broadcasted_iota(jnp.int32, (8, KEYS), 0)
+    scales[...] = jnp.where(head == 0, cos_scale[0], cos_scale[1])
+    for part in range(3):
+        columns = slice(part * MODEL, (part + 1) * MODEL)
+        weights[columns, :] = w_qkv[:, columns]
+    weights[3 * MODEL :, :] = w_out[...]
+
+    core, first_row, first_col = place_here()
+    spots = jnp.where(core == 0, key_spots[0], key_spots[1])
+    key_rows, key_cols = spots[0:1, :], spots[1:2, :]
+    turn = lax.broadcasted_iota(jnp.int32, (16, MODEL), 0)
+    turn = jnp.where(turn == lax.broadcasted_iota(jnp.int32, (16, MODEL), 1), 1.0, 0.0)
+    query_spots = dot_tn(spots[:, :NEAR].astype(BF16), turn.astype(BF16))
+    all_rows = key_rows + first_row.astype(F32)
+    all_cols = key_cols + first_col.astype(F32)
+    inside = (all_rows >= 0) & (all_rows < 128) & (all_cols >= 0) & (all_cols < 512)
+    key_rows = jnp.where(inside, key_rows, FAR_AWAY)
+    for start in range(0, QUERIES, BLOCK):
+        here = query_spots[start : start + BLOCK, :]
+        apart = jnp.maximum(
+            jnp.abs(here[:, 0:1] - key_rows), jnp.abs(here[:, 1:2] - key_cols)
+        )
+        bias[start : start + BLOCK, :] = jnp.where(apart <= RADIUS, 0.0, -1e30)
+
+
 def attention_kernel(
-    place,
-    cos_scale,
-    feat,
-    cot,
+    scales,
+    tile,
+    weights,
     mate,
     next_chip,
     far,
+    far_skip,
+    far_next,
     far_mate,
-    far_next,
-    far_skip,
-    w_qkv,
-    w_out,
-    key_spots,
-    query_spots,
+    bias,
     grad_feat,
     grad_w,
     grad_scale,
@@ -148,14 +178,16 @@
     d_attn,
     raw,
     dots,
-    bias,
     mix_own,
     mix_key,
     slope_own,
     slope_key,
 ):
-    core = place[0]
+    core, _, _ = place_here()
     other = 1 - core
+    w_query, w_key, w_value, w_out = (
+        weights[start : start + MODEL, :] for start in range(0, 4 * MODEL, MODEL)
+    )
     far_wide = far[...].astype(F32)
     mate_wide = far_mate[...].astype(F32)
     next_wide = far_next[0:SENT, :].astype(F32)
@@ -173,7 +205,7 @@
         pieces = [edge[kind * EDGE : (kind + 1) * EDGE] for edge in chosen]
         return jnp.concatenate(pieces, axis=0).astype(BF16)
 
-    tokens[0:128, :] = feat[...]
+    tokens[0:128, :] = tile[0:OWN, :]
     tokens[128:176, :] = rows_at(mate, 80 * core, 48)
     tokens[176:272, :] = strip(0, edges[:4])
     tokens[272:320, :] = rows_at(next_chip, 80 * other, 48)
@@ -183,29 +215,16 @@
     tokens[512:560, :] = rows_at(next_chip, 48 - 16 * other, 48)
     tokens[560:608, :] = strip(1, edges[4:])
     tokens[608:640, :] = jnp.zeros((32, MODEL), BF16)
-    cots[0:128, :] = cot[...]
+    cots[0:128, :] = tile[OWN:, :]
     cots[128:176, :] = rows_at(mate, OWN + 80 * core, 48)
     cots[176:272, :] = strip(2, edges[:4])
     cots[272:320, :] = rows_at(next_chip, OWN + 80 * other, 48)
     cots[320:368, :] = strip(2, edges[4:])
 
-    keys[...] = dot_nn(tokens[...], w_qkv[:, MODEL : 2 * MODEL]).astype(BF16)
-    values[...] = dot_nn(tokens[...], w_qkv[:, 2 * MODEL :]).astype(BF16)
-    queries[...] = dot_nn(tokens[0:QUERIES, :], w_qkv[:, :MODEL]).astype(BF16)
-    d_attn[...] = dot_nt(cots[...], w_out[...]).astype(BF16)
-
-    spots = key_spots[pl.ds(core, 1)].reshape(8, KEYS)
-    key_rows, key_cols = spots[0:1, :], spots[1:2, :]
-    all_rows = key_rows + place[1].astype(F32)
-    all_cols = key_cols + place[2].astype(F32)
-    inside = (all_rows >= 0) & (all_rows < 128) & (all_cols >= 0) & (all_cols < 512)
-    key_rows = jnp.where(inside, key_rows, FAR_AWAY)
-    for start in range(0, QUERIES, BLOCK):
-        here = query_spots[pl.ds(core, 1), start : start + BLOCK, :].reshape(BLOCK, 8)
-        apart = jnp.maximum(
-            jnp.abs(here[:, 0:1] - key_rows), jnp.abs(here[:, 1:2] - key_cols)
-        )
-        bias[start : start + BLOCK, :] = jnp.where(apart <= RADIUS, 0.0, -1e30)
+    keys[...] = dot_nn(tokens[...], w_key).astype(BF16)
+    values[...] = dot_nn(tokens[...], w_value).astype(BF16)
+    queries[...] = dot_nn(tokens[0:QUERIES, :], w_query).astype(BF16)
+    d_attn[...] = dot_nt(cots[...], w_out).astype(BF16)
 
     key_wide = keys[...].astype(F32)
     square = key_wide * key_wide
@@ -229,6 +248,9 @@
         raw[head] = dot_nt(jnp.where(own_lanes, queries[...], 0.0).astype(BF16), keys[...])
         dots[head] = dot_nt(jnp.where(own_lanes, d_attn[...], 0.0).astype(BF16), values[...])
 
+    key_inv = [key_inverse[head : head + 1, :] for head in range(2)]
+    key_reach = [key_inv[head] * scales[head : head + 1, :] for head in range(2)]
+    scale_lanes = jnp.where(first, scales[0:1, :MODEL], scales[1:2, :MODEL])
     scale_sums = [jnp.zeros((BLOCK, 1), F32), jnp.zeros((BLOCK, 1), F32)]
     for start in range(0, QUERIES, BLOCK):
         rows = slice(start, start + BLOCK)
@@ -236,9 +258,7 @@
         norms = head_sums(query_wide * query_wide)
         for head in range(2):
             inverse = lax.rsqrt(norms[head] + EPSILON)
-            reach = inverse * cos_scale[head]
-            key_inv = key_inverse[head : head + 1, :]
-            score = raw[head, rows, :] * (reach * LOG2E) * key_inv + bias[rows, :]
+            score = raw[head, rows, :] * (inverse * LOG2E) * key_reach[head] + bias[rows, :]
             expo = jnp.exp2(score)
             gain = dots[head, rows, :]
             share = 1.0 / (jnp.sum(expo, axis=1, keepdims=True) + 1e-30)
@@ -246,26 +266,26 @@
             if start < OWN:
                 weight = expo[:, :NEAR] * share
                 slope = weight * (gain[:, :NEAR] - center)
-                pull = slope * key_inv[:, :NEAR]
+                pull = slope * key_inv[head][:, :NEAR]
                 scale_sums[head] += inverse * jnp.sum(
                     pull * raw[head, rows, :NEAR], axis=1, keepdims=True
                 )
                 mix_own[head, rows, :] = weight.astype(BF16)
-                slope_own[head, rows, :] = (pull * cos_scale[head]).astype(BF16)
+                slope_own[head, rows, :] = pull.astype(BF16)
                 weight = weight[:, :OWN]
                 slope = slope[:, :OWN]
             else:
                 weight = expo[:, :OWN] * share
                 slope = weight * (gain[:, :OWN] - center)
             mix_key[head, rows, :] = weight.astype(BF16)
-            slope_key[head, rows, :] = (slope * reach).astype(BF16)
+            slope_key[head, rows, :] = (slope * inverse).astype(BF16)
 
     def both(dot, left, right):
         return jnp.where(first, dot(left[0], right), dot(left[1], right))
 
     attn_out = both(dot_nn, mix_own, values[0:NEAR, :]).astype(BF16)
-    dq_unit = both(dot_nn, slope_own, keys[0:NEAR, :])
-    dk_unit = both(dot_tn, slope_key, queries[...])
+    dq_unit = scale_lanes * both(dot_nn, slope_own, keys[0:NEAR, :])
+    dk_unit = scale_lanes * both(dot_tn, slope_key, queries[...])
     dv = both(dot_tn, mix_key, d_attn[...])
 
     def unit_backward(vector, grad_unit):
@@ -279,26 +299,38 @@
     dk = unit_backward(keys[0:OWN, :].astype(F32), dk_unit).astype(BF16)
     dv = dv.astype(BF16)
     grad_feat[...] = (
-        dot_nt(dq, w_qkv[:, :MODEL])
-        + dot_nt(dk, w_qkv[:, MODEL : 2 * MODEL])
-        + dot_nt(dv, w_qkv[:, 2 * MODEL :])
+        dot_nt(dq, w_query)
+        + dot_nt(dk, w_key)
+        + dot_nt(dv, w_value)
     ).astype(BF16)
     norm = 1.0 / 256.0
     for part, grad in enumerate((dq, dk, dv)):
         grad_w[part * MODEL : (part + 1) * MODEL, :] = (
-            dot_tn(feat[...], grad) * norm
+            dot_tn(tile[0:OWN, :], grad) * norm
         ).astype(BF16)
-    grad_w[3 * MODEL :, :] = (dot_tn(attn_out, cot[...]) * norm).astype(BF16)
+    grad_w[3 * MODEL :, :] = (dot_tn(attn_out, tile[OWN:, :]) * norm).astype(BF16)
 
     lane = lax.broadcasted_iota(jnp.int32, (8, MODEL), 1)
+    part = lax.broadcasted_iota(jnp.int32, (8, MODEL), 0)
+    terms = [jnp.sum(total, axis=0, keepdims=True) * norm for total in scale_sums]
+    rest = jnp.where(lane == 0, terms[0], jnp.where(lane == 1, terms[1], 0.0))
     held = jnp.zeros((8, MODEL), F32)
+    for which in range(3):
+        piece = rest.astype(BF16).astype(F32)
+        held = jnp.where(part == which, piece, held)
+        rest = rest - piece
+    grad_scale[...] = held.astype(BF16)
+
+
+def result_kernel(whole, share, grad_w_qkv, grad_w_out, grad_scale):
+    for part in range(3):
+        rows = slice(part * MODEL, (part + 1) * MODEL)
+        grad_w_qkv[:, rows] = whole[rows, :].astype(F32)
+    grad_w_out[...] = whole[3 * MODEL :, :].astype(F32)
+    total = jnp.sum(share[16:24, :], axis=0, keepdims=True)
+    lane = lax.broadcasted_iota(jnp.int32, (1, MODEL), 1)
     for head in range(2):
-        rest = jnp.sum(scale_sums[head], axis=0, keepdims=True) * norm
-        for part in range(3):
-            piece = rest.astype(BF16).astype(F32)
-            held = jnp.where(lane == 3 * head + part, piece, held)
-            rest = rest - piece
-    grad_scale[...] = held.astype(BF16)
+        grad_scale[head] = jnp.sum(jnp.where(lane == head, total, 0.0))
 
 
 def pairs(target):
@@ -349,32 +381,47 @@
 
 
 def on_device(features, cotangent, w_qkv, w_out, cos_scale):
-    row, col = lax.axis_index("row"), lax.axis_index("col")
-    place = jnp.stack([row % 2, row // 2 * 16, col * 16]).astype(jnp.int32)
     feat = features.reshape(OWN, MODEL)
     cot = cotangent.reshape(OWN, MODEL)
     smem = pl.BlockSpec(memory_space=pltpu.SMEM)
 
     edge = jax.ShapeDtypeStruct((SENT, MODEL), BF16)
-    own_edge, mate_edge, tile = pl.pallas_call(
+    tile = jnp.concatenate([feat, cot])
+    own_edge, mate_edge = pl.pallas_call(
         edge_kernel,
-        out_shape=(edge, edge, jax.ShapeDtypeStruct((2 * OWN, MODEL), BF16)),
-        in_specs=[smem] + vmem(2),
-        out_specs=vmem(3),
+        out_shape=(edge, edge),
+        in_specs=vmem(1),
+        out_specs=vmem(2),
+        compiler_params=pltpu.CompilerParams(vmem_limit_bytes=2 * 1024 * 1024),
         name="edges",
-    )(place, feat, cot)
+    )(tile)
     other_edge = lax.ppermute(mate_edge, EVERY, CHIP_MATE)
     far = lax.ppermute(jnp.concatenate([own_edge, other_edge]), EVERY, FAR_MATE)
-    mate = lax.ppermute(tile, EVERY, CHIP_MATE)
-    next_chip = lax.ppermute(tile, EVERY, NEXT_CHIP)
+    key_spots = np.zeros((2, 16, KEYS), np.float32)
+    key_spots[:, :2] = TABLES
+    key_spots = jnp.asarray(key_spots)
+    tile_copy, weights, bias, scales = pl.pallas_call(
+        prepare_kernel,
+        out_shape=(
+            jax.ShapeDtypeStruct((2 * OWN, MODEL), BF16),
+            jax.ShapeDtypeStruct((4 * MODEL, MODEL), BF16),
+            jax.ShapeDtypeStruct((QUERIES, KEYS), F32),
+            jax.ShapeDtypeStruct((8, KEYS), F32),
+        ),
+        in_specs=[smem] + vmem(5),
+        out_specs=vmem(4),
+        compiler_params=pltpu.CompilerParams(vmem_limit_bytes=4 * 1024 * 1024),
+        cost_estimate=pl.CostEstimate(
+            flops=1000000, bytes_accessed=1 << 20, transcendentals=0
+        ),
+        name="prepare",
+    )(cos_scale, tile, other_edge, w_qkv, w_out, key_spots)
+    mate = lax.ppermute(tile_copy, EVERY, CHIP_MATE)
+    next_chip = lax.ppermute(tile_copy, EVERY, NEXT_CHIP)
+
     far_mate = lax.ppermute(far, EVERY, CHIP_MATE)
     far_next = lax.ppermute(far, EVERY, NEXT_CHIP)
     far_skip = lax.ppermute(far, EVERY, SKIP_CHIP)
-
-    key_spots = np.zeros((2, 8, KEYS), np.float32)
-    key_spots[:, :2] = TABLES
-    query_spots = np.zeros((2, QUERIES, 8), np.float32)
-    query_spots[:, :, :2] = TABLES[:, :, :QUERIES].transpose(0, 2, 1)
     grad_feat, grad_w, scale_tile = pl.pallas_call(
         attention_kernel,
         out_shape=(
@@ -382,7 +429,7 @@
             jax.ShapeDtypeStruct((4 * MODEL, MODEL), BF16),
             jax.ShapeDtypeStruct((8, MODEL), BF16),
         ),
-        in_specs=[smem, smem] + vmem(12),
+        in_specs=vmem(10),
         out_specs=vmem(3),
         scratch_shapes=[
             pltpu.VMEM((KEYS, MODEL), BF16),
@@ -393,47 +440,49 @@
             pltpu.VMEM((QUERIES, MODEL), BF16),
             pltpu.VMEM((2, QUERIES, KEYS), F32),
             pltpu.VMEM((2, QUERIES, KEYS), F32),
-            pltpu.VMEM((QUERIES, KEYS), F32),
             pltpu.VMEM((2, OWN, NEAR), BF16),
             pltpu.VMEM((2, QUERIES, OWN), BF16),
             pltpu.VMEM((2, OWN, NEAR), BF16),
             pltpu.VMEM((2, QUERIES, OWN), BF16),
         ],
-        compiler_params=pltpu.CompilerParams(vmem_limit_bytes=32 * 1024 * 1024),
+        compiler_params=pltpu.CompilerParams(vmem_limit_bytes=16 * 1024 * 1024),
         name="window_attention",
     )(
-        place,
-        cos_scale,
-        feat,
-        cot,
+        scales,
+        tile,
+        weights,
         mate,
         next_chip,
         far,
+        far_skip,
+        far_next,
         far_mate,
-        far_next,
-        far_skip,
-        w_qkv,
-        w_out,
-        jnp.asarray(key_spots),
-        jnp.asarray(query_spots),
+        bias,
     )
 
     scale_rows = jnp.broadcast_to(scale_tile[None], (SHARES, 8, MODEL))
     shares = jnp.concatenate([grad_w.reshape(SHARES, 16, MODEL), scale_rows], axis=1)
     share = jnp.sum(exchange(shares, PLANES).astype(F32), axis=0)
-    pieces = share[16:17, 0:6].reshape(2, 3)
-    scale_part = jnp.sum(pieces, axis=1, keepdims=True)
-    top = lax.reduce_precision(scale_part, 8, 7)
-    middle = lax.reduce_precision(scale_part - top, 8, 7)
-    split = jnp.concatenate([top, middle, scale_part - top - middle], axis=1)
-    split = jnp.pad(split.reshape(1, 6), ((0, 7), (0, MODEL - 6)))
-    share = jnp.concatenate([share[:16], split], axis=0).astype(BF16)
+    scale_row = jnp.sum(share[16:19], axis=0, keepdims=True)
+    top = lax.reduce_precision(scale_row, 8, 7)
+    middle = lax.reduce_precision(scale_row - top, 8, 7)
+    split = [share[:16], top, middle, scale_row - top - middle, jnp.zeros((5, MODEL), F32)]
+    share = jnp.concatenate(split, axis=0).astype(BF16)
     share = jnp.sum(to_all(share, LINES).astype(F32), axis=0)
-    grad_scale = jnp.sum(share[16, 0:6].reshape(2, 3), axis=1)
-    whole = to_all(share[:16].astype(BF16), PLANES).astype(F32)
-    whole = whole.reshape(4, MODEL, MODEL)
-    grad_w_qkv = jnp.concatenate([whole[0], whole[1], whole[2]], axis=1)
-    return (grad_feat.reshape(ROWS, COLS, MODEL), grad_w_qkv, whole[3], grad_scale)
+    whole = to_all(share[:16].astype(BF16), PLANES).reshape(4 * MODEL, MODEL)
+    grad_w_qkv, grad_w_out, grad_scale = pl.pallas_call(
+        result_kernel,
+        out_shape=(
+            jax.ShapeDtypeStruct((MODEL, 3 * MODEL), F32),
+            jax.ShapeDtypeStruct((MODEL, MODEL), F32),
+            jax.ShapeDtypeStruct((2,), F32),
+        ),
+        in_specs=vmem(2),
+        out_specs=vmem(2) + [smem],
+        compiler_params=pltpu.CompilerParams(vmem_limit_bytes=2 * 1024 * 1024),
+        name="results",
+    )(whole, share)
+    return (grad_feat.reshape(ROWS, COLS, MODEL), grad_w_qkv, grad_w_out, grad_scale)
 
 
 def solution(mesh):

time: 90.4 us -> 82.5 us (0.913)
  blocking collectives: 31.3 us -> 41.9 us
  starting transfers between devices: 41.5 us -> 31.9 us
  local copies, waits for them, and re-layouts: 4.16 us -> 0.12 us
  waiting for transfers between devices: 4.18 us -> 1.98 us
  other arithmetic: 2.91 us -> 0.93 us
    all_to_all x2 -> x3, blocking collectives: 31.3 us -> 41.9 us  [exchange(): lax.all_to_all(array, EVERY, 0, 0, axis_index_groups=groups, tiled=True)]
    all_to_all x1 -> x0, starting transfers between devices: 9.72 us -> none  [exchange(): lax.all_to_all(array, EVERY, 0, 0, axis_index_groups=groups, tiled=True)]
    unnamed x16 -> x8, local copies, waits for them, and re-layouts: 2.4 us -> 0.02 us
    all_to_all x1 -> x0, waiting for transfers between devices: 1.99 us -> none  [exchange(): lax.all_to_all(array, EVERY, 0, 0, axis_index_groups=groups, tiled=True)]
    pallas_call x1 -> x3, Pallas kernels: 1.61 us -> 1.91 us  [the longest x1 1.02 us: on_device(): pl.pallas_call(prepare_kernel, out_shape=(jax.ShapeDtypeStruct((2 * OWN,...]
  transfers between devices with their start and end apart: 8 -> 7, of which waited for: 3 -> 2; matrix products, arithmetic and copies ran while one was open for 1% -> 0% of each run, Pallas kernels for 0% -> 1%
where the time goes in v3:
time: 82.5 us; the launch traced here: 82 us
  blocking collectives  41.9 us (51%)
  starting transfers between devices  31.9 us (39%)
  Pallas kernels  4.4 us (5%)
  waiting for transfers between devices  1.98 us (2%)
  other arithmetic  0.93 us (1%)
  between operations  0.83 us (1%)
    all_to_all x3, blocking collectives, exchange(): lax.all_to_all(array, EVERY, 0, 0, axis_index_groups=groups, tiled=True)  41.9 us
    ppermute x1, starting transfers between devices, on_device(): mate = lax.ppermute(tile_copy, EVERY, CHIP_MATE)  11.3 us
    ppermute x1, starting transfers between devices, on_device(): other_edge = lax.ppermute(mate_edge, EVERY, CHIP_MATE)  8.79 us
    ppermute x1, starting transfers between devices, on_device(): far_next = lax.ppermute(far, EVERY, NEXT_CHIP)  4.65 us
    ppermute x1, starting transfers between devices, on_device(): next_chip = lax.ppermute(tile_copy, EVERY, NEXT_CHIP)  2.54 us
    pallas_call x1, Pallas kernels, on_device(): pl.pallas_call(attention_kernel, out_shape=(jax.ShapeDtypeStruct((OWN, MO...  2.48 us
    ppermute x1, starting transfers between devices, on_device(): far_mate = lax.ppermute(far, EVERY, CHIP_MATE)  1.92 us
  transfers between devices with their start and end apart: 7, of which 2 were waited for; matrix products, arithmetic and copies ran while one was open for 0% of the time, Pallas kernels for 1%

profile of v3, /device:TPU:1, one launch (start us, length us, event | category | flops | bytes accessed | tf_op | source)
XLA Modules:
  0.0 82.0 jit_solution(12309394002240633502)
XLA Ops:
  0.6 0.0 copy-start.1
  0.6 0.8 pad_maximum_fusion.1.tile
  1.5 0.0 copy-start
  1.5 0.2 edges.1
  1.6 8.8 %collective-permute-start = (bf16[80,128]{1,0:T(8,128)(2,1)S(1)}, bf16[80,128]{1,0:T(8,128)(2,1)S(1)}, u32[]{:S(2)}, u32[]{:S(2)}) collective-permute-start(bf16[80,128]{1,0:T(8,128)(2,1)S(1)} %get-tuple-element.16), channel_id=1, source_target_pairs={{0,32},{1,33},{2,34},{3,35},{4,36},{5,37},{6,38},{7,39},{8,40},{9,... | collective-permute-start | bytes 61448 | tf_op jit(solution)/shard_map/ppermute | solution.py:398
  10.4 0.8 %collective-permute-done._ = bf16[80,128]{1,0:T(8,128)(2,1)S(1)} collective-permute-done((bf16[80,128]{1,0:T(8,128)(2,1)S(1)}, bf16[80,128]{1,0:T(8,128)(2,1)S(1)}, u32[]{:S(2)}, u32[]{:S(2)}) %collective-permute-start) | collective-permute-done | bytes 20512 | tf_op jit(solution)/shard_map/ppermute | solution.py:398
  11.3 0.0 copy-start.2
  11.3 0.0 copy-start.3
  11.3 1.4 %collective-permute-start.3 = (bf16[160,128]{1,0:T(8,128)(2,1)S(1)}, bf16[160,128]{1,0:T(8,128)(2,1)S(1)}, u32[]{:S(2)}, u32[]{:S(2)}) collective-permute-start(bf16[160,128]{1,0:T(8,128)(2,1)S(1)} %pad_maximum_fusion.2), channel_id=1, source_target_pairs={{0,1},{1,2},{2,3},{3,4},{4,5},{5,6},{6,7},{7,8},{8,9},{9,10},{10,1... | collective-permute-start | bytes 122888 | tf_op jit(solution)/shard_map/ppermute | solution.py:399
  12.7 0.0 copy-done.1
  12.7 0.0 copy-done
  12.7 0.0 copy-done.2
  12.7 0.0 copy-done.3
  12.7 1.0 %prepare.1 = (bf16[256,128]{1,0:T(8,128)(2,1)S(1)}, bf16[512,128]{1,0:T(8,128)(2,1)S(1)}, f32[368,640]{1,0:T(8,128)S(1)}, f32[8,640]{1,0:T(8,128)S(1)}) custom-call(f32[2]{0:T(128)S(1)} %copy-done.3, bf16[256,128]{1,0:T(8,128)(2,1)S(1)} %pad_maximum_fusion.1.tile, bf16[80,128]{1,0:T(8,128)(2,1)S(1)} %collective-permute-done._, bf16[128,384]{1,0:T(8,128)(2,1)S(1)} %copy-done, ...), custom_call_target="tpu_custom_call" | custom-call | flops 1000000 | bytes 1048576 | tf_op jit(solution)/shard_map/prepare/pallas_call | solution.py:403
  13.8 11.3 %collective-permute-start.1 = (bf16[256,128]{1,0:T(8,128)(2,1)S(1)}, bf16[256,128]{1,0:T(8,128)(2,1)S(1)}, u32[]{:S(2)}, u32[]{:S(2)}) collective-permute-start(bf16[256,128]{1,0:T(8,128)(2,1)S(1)} %get-tuple-element.19), channel_id=1, source_target_pairs={{0,32},{1,33},{2,34},{3,35},{4,36},{5,37},{6,38},{7,39},{8,40},{9,... | collective-permute-start | bytes 196616 | tf_op jit(solution)/shard_map/ppermute | solution.py:419
  25.1 2.5 %collective-permute-start.2 = (bf16[256,128]{1,0:T(8,128)(2,1)S(1)}, bf16[256,128]{1,0:T(8,128)(2,1)S(1)}, u32[]{:S(2)}, u32[]{:S(2)}) collective-permute-start(bf16[256,128]{1,0:T(8,128)(2,1)S(1)} %get-tuple-element.19), channel_id=1, source_target_pairs={{32,64},{33,65},{34,66},{35,67},{36,68},{37,69},{38,70},{39,71},{4... | collective-permute-start | bytes 196616 | tf_op jit(solution)/shard_map/ppermute | solution.py:420
  27.6 0.0 collective-permute-done.3.far
  27.6 1.3 %collective-permute-start.4 = (bf16[160,128]{1,0:T(8,128)(2,1)S(1)}, bf16[160,128]{1,0:T(8,128)(2,1)S(1)}, u32[]{:S(2)}, u32[]{:S(2)}) collective-permute-start(bf16[160,128]{1,0:T(8,128)(2,1)S(1)} %collective-permute-done.3.far), channel_id=1, source_target_pairs={{0,64},{1,65},{2,66},{3,67},{4,68},{5,69},{6,70},{7,71},{8,72},{9,... | collective-permute-start | bytes 122888 | tf_op jit(solution)/shard_map/ppermute | solution.py:424
  28.9 4.7 %collective-permute-start.5 = (bf16[160,128]{1,0:T(8,128)(2,1)S(1)}, bf16[160,128]{1,0:T(8,128)(2,1)S(1)}, u32[]{:S(2)}, u32[]{:S(2)}) collective-permute-start(bf16[160,128]{1,0:T(8,128)(2,1)S(1)} %collective-permute-done.3.far), channel_id=1, source_target_pairs={{32,64},{33,65},{34,66},{35,67},{36,68},{37,69},{38,70},{39,71},{4... | collective-permute-start | bytes 122888 | tf_op jit(solution)/shard_map/ppermute | solution.py:423
  33.6 1.9 %collective-permute-start.6 = (bf16[160,128]{1,0:T(8,128)(2,1)S(1)}, bf16[160,128]{1,0:T(8,128)(2,1)S(1)}, u32[]{:S(2)}, u32[]{:S(2)}) collective-permute-start(bf16[160,128]{1,0:T(8,128)(2,1)S(1)} %collective-permute-done.3.far), channel_id=1, source_target_pairs={{0,32},{1,33},{2,34},{3,35},{4,36},{5,37},{6,38},{7,39},{8,40},{9,... | collective-permute-start | bytes 122888 | tf_op jit(solution)/shard_map/ppermute | solution.py:422
  35.5 0.0 collective-permute-done.1.mate
  35.5 0.0 collective-permute-done.2.next_chip
  35.6 0.0 collective-permute-done.4.far_skip
  35.6 0.0 collective-permute-done.5.far_next
  35.6 1.1 %collective-permute-done.6.far_mate = bf16[160,128]{1,0:T(8,128)(2,1)S(1)} collective-permute-done((bf16[160,128]{1,0:T(8,128)(2,1)S(1)}, bf16[160,128]{1,0:T(8,128)(2,1)S(1)}, u32[]{:S(2)}, u32[]{:S(2)}) %collective-permute-start.6) | collective-permute-done | bytes 40992 | tf_op jit(solution)/shard_map/ppermute | solution.py:422
  36.7 2.5 %window_attention.1 = (bf16[128,128]{1,0:T(8,128)(2,1)}, bf16[512,128]{1,0:T(8,128)(2,1)S(1)}, bf16[8,128]{1,0:T(8,128)(2,1)S(1)}) custom-call(f32[8,640]{1,0:T(8,128)S(1)} %get-tuple-element.17.scales, bf16[256,128]{1,0:T(8,128)(2,1)S(1)} %pad_maximum_fusion.1.tile, bf16[512,128]{1,0:T(8,128)(2,1)S(1)} %get-tuple-element.18.weights, ...), custom_call_target="tpu_custom_call" | custom-call | tf_op jit(solution)/shard_map/window_attention/pallas_call | solution.py:425
  39.2 13.2 %all_to_all.15 = bf16[32,24,128]{2,1,0:T(8,128)(2,1)S(1)} all-to-all(bf16[32,24,128]{2,1,0:T(8,128)(2,1)S(1)} %pad_maximum_fusion), channel_id=1, replica_groups={{20,52,22,54,16,48,18,50,28,60,30,62,24,56,26,58,4,36,6,38,0,32,2,34,12..., dimensions={0} | all-to-all | bytes 393216 | tf_op jit(solution)/shard_map/all_to_all | solution.py:376
  52.6 16.9 %all_to_all.16 = bf16[16,24,128]{2,1,0:T(8,128)(2,1)S(1)} all-to-all(bf16[16,24,128]{2,1,0:T(8,128)(2,1)S(1)} %broadcast_in_dim.10), channel_id=1, replica_groups={{1,65,129,193,257,321,385,449,0,64,128,192,256,320,384,448},{33,97,161,..., dimensions={0} | all-to-all | bytes 196608 | tf_op jit(solution)/shard_map/all_to_all | solution.py:376
  69.6 11.7 %all_to_all.17 = bf16[32,16,128]{2,1,0:T(8,128)(2,1)S(1)} all-to-all(bf16[32,16,128]{2,1,0:T(8,128)(2,1)S(1)} %broadcast_in_dim.11), channel_id=1, replica_groups={{20,52,22,54,16,48,18,50,28,60,30,62,24,56,26,58,4,36,6,38,0,32,2,34,12..., dimensions={0} | all-to-all | bytes 262144 | tf_op jit(solution)/shard_map/all_to_all | solution.py:376
  81.3 0.7 results.1
  (13 shorter events, 0.2 us)
Async XLA Ops:
  0.6 12.1 %copy-start.1 = (f32[2,16,640]{2,1,0:T(8,128)S(1)}, f32[2,16,640]{2,1,0:T(8,128)}, u32[]{:S(2)}) copy-start(f32[2,16,640]{2,1,0:T(8,128)} %constant.7.clone.key_spots) | copy-start | bytes 245764
  1.5 11.2 %copy-start = (bf16[128,384]{1,0:T(8,128)(2,1)S(1)}, bf16[128,384]{1,0:T(8,128)(2,1)}, u32[]{:S(2)}) copy-start(bf16[128,384]{1,0:T(8,128)(2,1)} %w_qkv.1) | copy-start | bytes 294916
  1.6 9.6 %collective-permute-start = (bf16[80,128]{1,0:T(8,128)(2,1)S(1)}, bf16[80,128]{1,0:T(8,128)(2,1)S(1)}, u32[]{:S(2)}, u32[]{:S(2)}) collective-permute-start(bf16[80,128]{1,0:T(8,128)(2,1)S(1)} %get-tuple-element.16), channel_id=1, source_target_pairs={{0,32},{1,33},{2,34},{3,35},{4,36},{5,37},{6,38},{7,39},{8,40},{9,... | collective-permute-start | bytes 61448 | tf_op jit(solution)/shard_map/ppermute | solution.py:398
  11.3 1.5 %copy-start.2 = (bf16[128,128]{1,0:T(8,128)(2,1)S(1)}, bf16[128,128]{1,0:T(8,128)(2,1)}, u32[]{:S(2)}) copy-start(bf16[128,128]{1,0:T(8,128)(2,1)} %w_out.1) | copy-start | bytes 98308
  11.3 1.5 %copy-start.3 = (f32[2]{0:T(128)S(1)}, f32[2]{0:T(128)}, u32[]{:S(2)}) copy-start(f32[2]{0:T(128)} %cos_scale.1) | copy-start | bytes 28
  11.3 16.4 %collective-permute-start.3 = (bf16[160,128]{1,0:T(8,128)(2,1)S(1)}, bf16[160,128]{1,0:T(8,128)(2,1)S(1)}, u32[]{:S(2)}, u32[]{:S(2)}) collective-permute-start(bf16[160,128]{1,0:T(8,128)(2,1)S(1)} %pad_maximum_fusion.2), channel_id=1, source_target_pairs={{0,1},{1,2},{2,3},{3,4},{4,5},{5,6},{6,7},{7,8},{8,9},{9,10},{10,1... | collective-permute-start | bytes 122888 | tf_op jit(solution)/shard_map/ppermute | solution.py:399
  13.8 21.8 %collective-permute-start.1 = (bf16[256,128]{1,0:T(8,128)(2,1)S(1)}, bf16[256,128]{1,0:T(8,128)(2,1)S(1)}, u32[]{:S(2)}, u32[]{:S(2)}) collective-permute-start(bf16[256,128]{1,0:T(8,128)(2,1)S(1)} %get-tuple-element.19), channel_id=1, source_target_pairs={{0,32},{1,33},{2,34},{3,35},{4,36},{5,37},{6,38},{7,39},{8,40},{9,... | collective-permute-start | bytes 196616 | tf_op jit(solution)/shard_map/ppermute | solution.py:419
  25.1 10.5 %collective-permute-start.2 = (bf16[256,128]{1,0:T(8,128)(2,1)S(1)}, bf16[256,128]{1,0:T(8,128)(2,1)S(1)}, u32[]{:S(2)}, u32[]{:S(2)}) collective-permute-start(bf16[256,128]{1,0:T(8,128)(2,1)S(1)} %get-tuple-element.19), channel_id=1, source_target_pairs={{32,64},{33,65},{34,66},{35,67},{36,68},{37,69},{38,70},{39,71},{4... | collective-permute-start | bytes 196616 | tf_op jit(solution)/shard_map/ppermute | solution.py:420
  27.6 7.9 %collective-permute-start.4 = (bf16[160,128]{1,0:T(8,128)(2,1)S(1)}, bf16[160,128]{1,0:T(8,128)(2,1)S(1)}, u32[]{:S(2)}, u32[]{:S(2)}) collective-permute-start(bf16[160,128]{1,0:T(8,128)(2,1)S(1)} %collective-permute-done.3.far), channel_id=1, source_target_pairs={{0,64},{1,65},{2,66},{3,67},{4,68},{5,69},{6,70},{7,71},{8,72},{9,... | collective-permute-start | bytes 122888 | tf_op jit(solution)/shard_map/ppermute | solution.py:424
  28.9 6.6 %collective-permute-start.5 = (bf16[160,128]{1,0:T(8,128)(2,1)S(1)}, bf16[160,128]{1,0:T(8,128)(2,1)S(1)}, u32[]{:S(2)}, u32[]{:S(2)}) collective-permute-start(bf16[160,128]{1,0:T(8,128)(2,1)S(1)} %collective-permute-done.3.far), channel_id=1, source_target_pairs={{32,64},{33,65},{34,66},{35,67},{36,68},{37,69},{38,70},{39,71},{4... | collective-permute-start | bytes 122888 | tf_op jit(solution)/shard_map/ppermute | solution.py:423
  33.6 3.1 %collective-permute-start.6 = (bf16[160,128]{1,0:T(8,128)(2,1)S(1)}, bf16[160,128]{1,0:T(8,128)(2,1)S(1)}, u32[]{:S(2)}, u32[]{:S(2)}) collective-permute-start(bf16[160,128]{1,0:T(8,128)(2,1)S(1)} %collective-permute-done.3.far), channel_id=1, source_target_pairs={{0,32},{1,33},{2,34},{3,35},{4,36},{5,37},{6,38},{7,39},{8,40},{9,... | collective-permute-start | bytes 122888 | tf_op jit(solution)/shard_map/ppermute | solution.py:422

commit v4 on v3

--- a/solution.py
+++ b/solution.py
@@ -93,7 +93,7 @@
     return jnp.dot(left, right, preferred_element_type=F32)
 
 
-def edge_kernel(tile, own_edge, mate_edge):
+def edge_kernel(tile, own_edge, mate_message):
     core, _, _ = place_here()
     spot = lax.broadcasted_iota(jnp.int32, (SENT, 128), 0)
     token = lax.broadcasted_iota(jnp.int32, (SENT, 128), 1)
@@ -108,14 +108,18 @@
     from_cot = kind == 2
     for ref, wanted in (
         (own_edge, jnp.where(core == 0, right, left)),
-        (mate_edge, jnp.where(core == 0, left, right)),
+        (mate_message, jnp.where(core == 0, left, right)),
     ):
         hit = (wanted == token) & used
         of_feat = jnp.where(hit & ~from_cot, 1.0, 0.0).astype(BF16)
         of_cot = jnp.where(hit & from_cot, 1.0, 0.0).astype(BF16)
-        ref[...] = (
+        ref[0:SENT, :] = (
             dot_nn(of_feat, tile[0:OWN, :]) + dot_nn(of_cot, tile[OWN:, :])
         ).astype(BF16)
+    half = 1 - core
+    mate_message[SENT : SENT + 48, :] = rows_at(tile, 80 * half, 48)
+    mate_message[SENT + 48 : SENT + 96, :] = rows_at(tile, 48 - 16 * half, 48)
+    mate_message[SENT + 96 : SENT + 144, :] = rows_at(tile, OWN + 80 * half, 48)
 
 
 def place_here():
@@ -127,12 +131,8 @@
     return ref[pl.ds(pl.multiple_of(start, 16), count), :]
 
 
-def prepare_kernel(
-    cos_scale, tile, _, w_qkv, w_out, key_spots, tile_copy, weights, bias, scales
-):
+def prepare_kernel(tile, _, w_qkv, w_out, key_spots, tile_copy, weights, bias):
     tile_copy[...] = tile[...]
-    head = lax.broadcasted_iota(jnp.int32, (8, KEYS), 0)
-    scales[...] = jnp.where(head == 0, cos_scale[0], cos_scale[1])
     for part in range(3):
         columns = slice(part * MODEL, (part + 1) * MODEL)
         weights[columns, :] = w_qkv[:, columns]
@@ -206,17 +206,17 @@
         return jnp.concatenate(pieces, axis=0).astype(BF16)
 
     tokens[0:128, :] = tile[0:OWN, :]
-    tokens[128:176, :] = rows_at(mate, 80 * core, 48)
+    tokens[128:176, :] = mate[SENT : SENT + 48, :]
     tokens[176:272, :] = strip(0, edges[:4])
     tokens[272:320, :] = rows_at(next_chip, 80 * other, 48)
     tokens[320:368, :] = strip(0, edges[4:])
-    tokens[368:416, :] = rows_at(mate, 48 - 16 * core, 48)
+    tokens[368:416, :] = mate[SENT + 48 : SENT + 96, :]
     tokens[416:512, :] = strip(1, edges[:4])
     tokens[512:560, :] = rows_at(next_chip, 48 - 16 * other, 48)
     tokens[560:608, :] = strip(1, edges[4:])
     tokens[608:640, :] = jnp.zeros((32, MODEL), BF16)
     cots[0:128, :] = tile[OWN:, :]
-    cots[128:176, :] = rows_at(mate, OWN + 80 * core, 48)
+    cots[128:176, :] = mate[SENT + 96 : SENT + 144, :]
     cots[176:272, :] = strip(2, edges[:4])
     cots[272:320, :] = rows_at(next_chip, OWN + 80 * other, 48)
     cots[320:368, :] = strip(2, edges[4:])
@@ -313,24 +313,23 @@
     lane = lax.broadcasted_iota(jnp.int32, (8, MODEL), 1)
     part = lax.broadcasted_iota(jnp.int32, (8, MODEL), 0)
     terms = [jnp.sum(total, axis=0, keepdims=True) * norm for total in scale_sums]
-    rest = jnp.where(lane == 0, terms[0], jnp.where(lane == 1, terms[1], 0.0))
+    rest = jnp.where(part == 0, terms[0], terms[1])
     held = jnp.zeros((8, MODEL), F32)
     for which in range(3):
         piece = rest.astype(BF16).astype(F32)
-        held = jnp.where(part == which, piece, held)
+        held = jnp.where(lane == which, piece, held)
         rest = rest - piece
     grad_scale[...] = held.astype(BF16)
 
 
-def result_kernel(whole, share, grad_w_qkv, grad_w_out, grad_scale):
+def result_kernel(whole, terms, feat_tile, grad_feat, grad_w_qkv, grad_w_out, grad_scale):
+    grad_feat[...] = feat_tile[...]
     for part in range(3):
         rows = slice(part * MODEL, (part + 1) * MODEL)
         grad_w_qkv[:, rows] = whole[rows, :].astype(F32)
     grad_w_out[...] = whole[3 * MODEL :, :].astype(F32)
-    total = jnp.sum(share[16:24, :], axis=0, keepdims=True)
-    lane = lax.broadcasted_iota(jnp.int32, (1, MODEL), 1)
     for head in range(2):
-        grad_scale[head] = jnp.sum(jnp.where(lane == head, total, 0.0))
+        grad_scale[head] = jnp.sum(terms[head : head + 1, :])
 
 
 def pairs(target):
@@ -350,7 +349,7 @@
     return ((z % 8) * 2 + core) * 32 + (x % 4) * 8 + (y % 4) * 2 + z // 8 % 2
 
 
-FIRST_X, FIRST_Y, FIRST_Z = 2, 2, 8
+FIRST_X, FIRST_Y, FIRST_Z = 2, 2, 9
 PLANES = [
     [
         device(x + FIRST_X, y + FIRST_Y, z, core)
@@ -387,36 +386,36 @@
 
     edge = jax.ShapeDtypeStruct((SENT, MODEL), BF16)
     tile = jnp.concatenate([feat, cot])
-    own_edge, mate_edge = pl.pallas_call(
+    own_edge, mate_message = pl.pallas_call(
         edge_kernel,
-        out_shape=(edge, edge),
+        out_shape=(edge, jax.ShapeDtypeStruct((SENT + 144, MODEL), BF16)),
         in_specs=vmem(1),
         out_specs=vmem(2),
         compiler_params=pltpu.CompilerParams(vmem_limit_bytes=2 * 1024 * 1024),
         name="edges",
     )(tile)
-    other_edge = lax.ppermute(mate_edge, EVERY, CHIP_MATE)
+    mate = lax.ppermute(mate_message, EVERY, CHIP_MATE)
+    other_edge = mate[:SENT]
     far = lax.ppermute(jnp.concatenate([own_edge, other_edge]), EVERY, FAR_MATE)
     key_spots = np.zeros((2, 16, KEYS), np.float32)
     key_spots[:, :2] = TABLES
     key_spots = jnp.asarray(key_spots)
-    tile_copy, weights, bias, scales = pl.pallas_call(
+    scales = jnp.broadcast_to(cos_scale[None, :, None], (4, 2, KEYS)).reshape(8, KEYS)
+    tile_copy, weights, bias = pl.pallas_call(
         prepare_kernel,
         out_shape=(
             jax.ShapeDtypeStruct((2 * OWN, MODEL), BF16),
             jax.ShapeDtypeStruct((4 * MODEL, MODEL), BF16),
             jax.ShapeDtypeStruct((QUERIES, KEYS), F32),
-            jax.ShapeDtypeStruct((8, KEYS), F32),
         ),
-        in_specs=[smem] + vmem(5),
-        out_specs=vmem(4),
+        in_specs=vmem(5),
+        out_specs=vmem(3),
         compiler_params=pltpu.CompilerParams(vmem_limit_bytes=4 * 1024 * 1024),
         cost_estimate=pl.CostEstimate(
             flops=1000000, bytes_accessed=1 << 20, transcendentals=0
         ),
         name="prepare",
-    )(cos_scale, tile, other_edge, w_qkv, w_out, key_spots)
-    mate = lax.ppermute(tile_copy, EVERY, CHIP_MATE)
+    )(tile, mate, w_qkv, w_out, key_spots)
     next_chip = lax.ppermute(tile_copy, EVERY, NEXT_CHIP)
 
     far_mate = lax.ppermute(far, EVERY, CHIP_MATE)
@@ -460,28 +459,33 @@
         bias,
     )
 
-    scale_rows = jnp.broadcast_to(scale_tile[None], (SHARES, 8, MODEL))
-    shares = jnp.concatenate([grad_w.reshape(SHARES, 16, MODEL), scale_rows], axis=1)
+    scale_rows = jnp.broadcast_to(scale_tile[None, None, :2], (SHARES, 1, 2, MODEL))
+    shares = jnp.concatenate([grad_w.reshape(SHARES, 8, 2, MODEL), scale_rows], axis=1)
+    lane = lax.broadcasted_iota(jnp.int32, (2, MODEL), 1)
+    shares, lane = lax.optimization_barrier((shares, lane))
     share = jnp.sum(exchange(shares, PLANES).astype(F32), axis=0)
-    scale_row = jnp.sum(share[16:19], axis=0, keepdims=True)
-    top = lax.reduce_precision(scale_row, 8, 7)
-    middle = lax.reduce_precision(scale_row - top, 8, 7)
-    split = [share[:16], top, middle, scale_row - top - middle, jnp.zeros((5, MODEL), F32)]
-    share = jnp.concatenate(split, axis=0).astype(BF16)
+    term = jnp.sum(jnp.where(lane < 3, share[8], 0.0), axis=1, keepdims=True)
+    top = lax.reduce_precision(term, 8, 7)
+    middle = lax.reduce_precision(term - top, 8, 7)
+    parts = jnp.where(lane == 0, top, jnp.where(lane == 1, middle, term - top - middle))
+    parts = jnp.where(lane < 3, parts, 0.0)
+    share = jnp.concatenate([share[:8], parts[None]], axis=0).astype(BF16)
     share = jnp.sum(to_all(share, LINES).astype(F32), axis=0)
-    whole = to_all(share[:16].astype(BF16), PLANES).reshape(4 * MODEL, MODEL)
-    grad_w_qkv, grad_w_out, grad_scale = pl.pallas_call(
+    share, terms = lax.optimization_barrier((share[:8].astype(BF16).reshape(16, MODEL), share[8]))
+    whole = to_all(share, PLANES).reshape(4 * MODEL, MODEL)
+    grad_feat, grad_w_qkv, grad_w_out, grad_scale = pl.pallas_call(
         result_kernel,
         out_shape=(
+            jax.ShapeDtypeStruct((OWN, MODEL), BF16),
             jax.ShapeDtypeStruct((MODEL, 3 * MODEL), F32),
             jax.ShapeDtypeStruct((MODEL, MODEL), F32),
             jax.ShapeDtypeStruct((2,), F32),
         ),
-        in_specs=vmem(2),
-        out_specs=vmem(2) + [smem],
+        in_specs=vmem(3),
+        out_specs=vmem(3) + [smem],
         compiler_params=pltpu.CompilerParams(vmem_limit_bytes=2 * 1024 * 1024),
         name="results",
-    )(whole, share)
+    )(whole, terms, grad_feat)
     return (grad_feat.reshape(ROWS, COLS, MODEL), grad_w_qkv, grad_w_out, grad_scale)
 
 

time: 82.5 us -> 81 us (0.982)
  starting transfers between devices: 31.9 us -> 28.8 us
  blocking collectives: 41.9 us -> 44.1 us
  Pallas kernels: 4.4 us -> 3.27 us
    ppermute x2 -> x1, starting transfers between devices: 20.1 us -> 8.79 us  [on_device(): mate = lax.ppermute(mate_message, EVERY, CHIP_MATE)]
    ppermute x1, starting transfers between devices: 2.54 us -> 11.9 us  [on_device(): next_chip = lax.ppermute(tile_copy, EVERY, NEXT_CHIP)]
    all_to_all x3, blocking collectives: 41.9 us -> 44.1 us  [exchange(): lax.all_to_all(array, EVERY, 0, 0, axis_index_groups=groups, tiled=True)]
    ppermute x1, starting transfers between devices: 4.65 us -> 3.56 us  [on_device(): far_next = lax.ppermute(far, EVERY, NEXT_CHIP)]
  transfers between devices with their start and end apart: 7 -> 6, of which waited for: 2 -> 2; matrix products, arithmetic and copies ran while one was open for 0% -> 0% of each run, Pallas kernels for 1% -> 1%
where the time goes in v4:
time: 81 us; the launch traced here: 80.6 us
  blocking collectives  44.1 us (54%)
  starting transfers between devices  28.8 us (36%)
  Pallas kernels  3.27 us (4%)
  waiting for transfers between devices  1.95 us (2%)
  other arithmetic  1.38 us (2%)
  between operations  0.84 us (1%)
    all_to_all x3, blocking collectives, exchange(): lax.all_to_all(array, EVERY, 0, 0, axis_index_groups=groups, tiled=True)  44.1 us
    ppermute x1, starting transfers between devices, on_device(): next_chip = lax.ppermute(tile_copy, EVERY, NEXT_CHIP)  11.9 us
    ppermute x1, starting transfers between devices, on_device(): mate = lax.ppermute(mate_message, EVERY, CHIP_MATE)  8.79 us
    ppermute x1, starting transfers between devices, on_device(): far_next = lax.ppermute(far, EVERY, NEXT_CHIP)  3.56 us
    ppermute x1, starting transfers between devices, on_device(): far_mate = lax.ppermute(far, EVERY, CHIP_MATE)  1.92 us
    pallas_call x1, Pallas kernels, on_device(): pl.pallas_call(attention_kernel, out_shape=(jax.ShapeDtypeStruct((OWN, MO...  1.88 us
  transfers between devices with their start and end apart: 6, of which 2 were waited for; matrix products, arithmetic and copies ran while one was open for 0% of the time, Pallas kernels for 1%

profile of v4, /device:TPU:1, one launch (start us, length us, event | category | flops | bytes accessed | tf_op | source)
XLA Modules:
  0.0 80.6 jit_solution(668055693508372031)
XLA Ops:
  0.6 0.0 copy-start.2
  0.6 0.8 pad_maximum_fusion.1.tile
  1.4 0.2 edges.1
  1.6 8.8 %collective-permute-start = (bf16[224,128]{1,0:T(8,128)(2,1)S(1)}, bf16[224,128]{1,0:T(8,128)(2,1)S(1)}, u32[]{:S(2)}, u32[]{:S(2)}) collective-permute-start(bf16[224,128]{1,0:T(8,128)(2,1)S(1)} %get-tuple-element.20), channel_id=1, source_target_pairs={{0,32},{1,33},{2,34},{3,35},{4,36},{5,37},{6,38},{7,39},{8,40},{9,... | collective-permute-start | bytes 172040 | tf_op jit(solution)/shard_map/ppermute | solution.py:397
  10.4 0.9 %collective-permute-done._.mate = bf16[224,128]{1,0:T(8,128)(2,1)S(1)} collective-permute-done((bf16[224,128]{1,0:T(8,128)(2,1)S(1)}, bf16[224,128]{1,0:T(8,128)(2,1)S(1)}, u32[]{:S(2)}, u32[]{:S(2)}) %collective-permute-start) | collective-permute-done | bytes 57376 | tf_op jit(solution)/shard_map/ppermute | solution.py:397
  11.3 1.3 %collective-permute-start.2 = (bf16[160,128]{1,0:T(8,128)(2,1)S(1)}, bf16[160,128]{1,0:T(8,128)(2,1)S(1)}, u32[]{:S(2)}, u32[]{:S(2)}) collective-permute-start(bf16[160,128]{1,0:T(8,128)(2,1)S(1)} %pad_maximum_fusion.2), channel_id=1, source_target_pairs={{0,1},{1,2},{2,3},{3,4},{4,5},{5,6},{6,7},{7,8},{8,9},{9,10},{10,1... | collective-permute-start | bytes 122888 | tf_op jit(solution)/shard_map/ppermute | solution.py:399
  12.6 0.0 copy-done.2
  12.6 0.0 copy-done
  12.6 0.0 copy-done.1
  12.6 0.5 prepare.1
  13.1 0.0 copy-start.3
  13.1 11.9 %collective-permute-start.1 = (bf16[256,128]{1,0:T(8,128)(2,1)S(1)}, bf16[256,128]{1,0:T(8,128)(2,1)S(1)}, u32[]{:S(2)}, u32[]{:S(2)}) collective-permute-start(bf16[256,128]{1,0:T(8,128)(2,1)S(1)} %get-tuple-element.22), channel_id=1, source_target_pairs={{32,64},{33,65},{34,66},{35,67},{36,68},{37,69},{38,70},{39,71},{4... | collective-permute-start | bytes 196616 | tf_op jit(solution)/shard_map/ppermute | solution.py:419
  25.1 0.0 collective-permute-done.2.far
  25.1 1.3 %collective-permute-start.3 = (bf16[160,128]{1,0:T(8,128)(2,1)S(1)}, bf16[160,128]{1,0:T(8,128)(2,1)S(1)}, u32[]{:S(2)}, u32[]{:S(2)}) collective-permute-start(bf16[160,128]{1,0:T(8,128)(2,1)S(1)} %collective-permute-done.2.far), channel_id=1, source_target_pairs={{0,64},{1,65},{2,66},{3,67},{4,68},{5,69},{6,70},{7,71},{8,72},{9,... | collective-permute-start | bytes 122888 | tf_op jit(solution)/shard_map/ppermute | solution.py:423
  26.4 3.6 %collective-permute-start.4 = (bf16[160,128]{1,0:T(8,128)(2,1)S(1)}, bf16[160,128]{1,0:T(8,128)(2,1)S(1)}, u32[]{:S(2)}, u32[]{:S(2)}) collective-permute-start(bf16[160,128]{1,0:T(8,128)(2,1)S(1)} %collective-permute-done.2.far), channel_id=1, source_target_pairs={{32,64},{33,65},{34,66},{35,67},{36,68},{37,69},{38,70},{39,71},{4... | collective-permute-start | bytes 122888 | tf_op jit(solution)/shard_map/ppermute | solution.py:422
  29.9 1.9 %collective-permute-start.5 = (bf16[160,128]{1,0:T(8,128)(2,1)S(1)}, bf16[160,128]{1,0:T(8,128)(2,1)S(1)}, u32[]{:S(2)}, u32[]{:S(2)}) collective-permute-start(bf16[160,128]{1,0:T(8,128)(2,1)S(1)} %collective-permute-done.2.far), channel_id=1, source_target_pairs={{0,32},{1,33},{2,34},{3,35},{4,36},{5,37},{6,38},{7,39},{8,40},{9,... | collective-permute-start | bytes 122888 | tf_op jit(solution)/shard_map/ppermute | solution.py:421
  31.9 0.0 copy-done.3
  31.9 0.1 broadcast_in_dim.60
  32.0 0.0 collective-permute-done.1.next_chip
  32.0 0.0 collective-permute-done.3.far_skip
  32.0 0.0 collective-permute-done.4.far_next
  32.0 1.1 %collective-permute-done.5.far_mate = bf16[160,128]{1,0:T(8,128)(2,1)S(1)} collective-permute-done((bf16[160,128]{1,0:T(8,128)(2,1)S(1)}, bf16[160,128]{1,0:T(8,128)(2,1)S(1)}, u32[]{:S(2)}, u32[]{:S(2)}) %collective-permute-start.5) | collective-permute-done | bytes 40992 | tf_op jit(solution)/shard_map/ppermute | solution.py:421
  33.0 0.1 broadcast_in_dim.61.scales
  33.1 1.9 %window_attention.1 = (bf16[128,128]{1,0:T(8,128)(2,1)S(1)}, bf16[512,128]{1,0:T(8,128)(2,1)S(1)}, bf16[8,128]{1,0:T(8,128)(2,1)S(1)}) custom-call(f32[8,640]{1,0:T(8,128)S(1)} %broadcast_in_dim.61.scales, bf16[256,128]{1,0:T(8,128)(2,1)S(1)} %pad_maximum_fusion.1.tile, bf16[512,128]{1,0:T(8,128)(2,1)S(1)} %get-tuple-element.21.weights, ...), custom_call_target="tpu_custom_call" | custom-call | tf_op jit(solution)/shard_map/window_attention/pallas_call | solution.py:424
  35.0 0.2 pad_maximum_fusion
  35.3 13.9 %all_to_all.15 = bf16[32,9,2,128]{3,2,1,0:T(2,128)(2,1)S(1)} all-to-all(bf16[32,9,2,128]{3,2,1,0:T(2,128)(2,1)S(1)} %pad_maximum_fusion), channel_id=1, replica_groups={{20,52,22,54,16,48,18,50,28,60,30,62,24,56,26,58,4,36,6,38,0,32,2,34,12..., dimensions={0} | all-to-all | bytes 294912 | tf_op jit(solution)/shard_map/all_to_all | solution.py:375
  49.1 0.1 convert_reduce_fusion
  49.3 0.1 fusion.3
  49.4 0.1 fusion.4
  49.5 18.2 %all_to_all.16 = bf16[16,9,2,128]{3,2,1,0:T(2,128)(2,1)S(1)} all-to-all(bf16[16,9,2,128]{3,2,1,0:T(2,128)(2,1)S(1)} %broadcast_in_dim.67), channel_id=1, replica_groups={{65,129,193,257,321,385,449,0,64,128,192,256,320,384,448,1},{97,161,225..., dimensions={0} | all-to-all | bytes 147456 | tf_op jit(solution)/shard_map/all_to_all | solution.py:375
  67.8 12.1 %all_to_all.17 = bf16[32,16,128]{2,1,0:T(8,128)(2,1)S(1)} all-to-all(bf16[32,16,128]{2,1,0:T(8,128)(2,1)S(1)} %broadcast_in_dim.68), channel_id=1, replica_groups={{20,52,22,54,16,48,18,50,28,60,30,62,24,56,26,58,4,36,6,38,0,32,2,34,12..., dimensions={0} | all-to-all | bytes 262144 | tf_op jit(solution)/shard_map/all_to_all | solution.py:375
  79.9 0.7 results.1
  (16 shorter events, 0.2 us)
Async XLA Ops:
  0.6 11.9 %copy-start.2 = (bf16[128,128]{1,0:T(8,128)(2,1)S(1)}, bf16[128,128]{1,0:T(8,128)(2,1)}, u32[]{:S(2)}) copy-start(bf16[128,128]{1,0:T(8,128)(2,1)} %w_out.1) | copy-start | bytes 98308
  1.4 11.2 %copy-start = (bf16[128,384]{1,0:T(8,128)(2,1)S(1)}, bf16[128,384]{1,0:T(8,128)(2,1)}, u32[]{:S(2)}) copy-start(bf16[128,384]{1,0:T(8,128)(2,1)} %w_qkv.1) | copy-start | bytes 294916
  1.4 11.2 %copy-start.1 = (f32[2,16,640]{2,1,0:T(8,128)S(1)}, f32[2,16,640]{2,1,0:T(8,128)}, u32[]{:S(2)}) copy-start(f32[2,16,640]{2,1,0:T(8,128)} %constant.10.clone.key_spots) | copy-start | bytes 245764
  1.6 9.7 %collective-permute-start = (bf16[224,128]{1,0:T(8,128)(2,1)S(1)}, bf16[224,128]{1,0:T(8,128)(2,1)S(1)}, u32[]{:S(2)}, u32[]{:S(2)}) collective-permute-start(bf16[224,128]{1,0:T(8,128)(2,1)S(1)} %get-tuple-element.20), channel_id=1, source_target_pairs={{0,32},{1,33},{2,34},{3,35},{4,36},{5,37},{6,38},{7,39},{8,40},{9,... | collective-permute-start | bytes 172040 | tf_op jit(solution)/shard_map/ppermute | solution.py:397
  11.3 13.8 %collective-permute-start.2 = (bf16[160,128]{1,0:T(8,128)(2,1)S(1)}, bf16[160,128]{1,0:T(8,128)(2,1)S(1)}, u32[]{:S(2)}, u32[]{:S(2)}) collective-permute-start(bf16[160,128]{1,0:T(8,128)(2,1)S(1)} %pad_maximum_fusion.2), channel_id=1, source_target_pairs={{0,1},{1,2},{2,3},{3,4},{4,5},{5,6},{6,7},{7,8},{8,9},{9,10},{10,1... | collective-permute-start | bytes 122888 | tf_op jit(solution)/shard_map/ppermute | solution.py:399
  13.1 18.8 %copy-start.3 = (f32[2]{0:T(128)S(1)}, f32[2]{0:T(128)}, u32[]{:S(2)}) copy-start(f32[2]{0:T(128)} %param.10) | copy-start | bytes 28
  13.1 18.9 %collective-permute-start.1 = (bf16[256,128]{1,0:T(8,128)(2,1)S(1)}, bf16[256,128]{1,0:T(8,128)(2,1)S(1)}, u32[]{:S(2)}, u32[]{:S(2)}) collective-permute-start(bf16[256,128]{1,0:T(8,128)(2,1)S(1)} %get-tuple-element.22), channel_id=1, source_target_pairs={{32,64},{33,65},{34,66},{35,67},{36,68},{37,69},{38,70},{39,71},{4... | collective-permute-start | bytes 196616 | tf_op jit(solution)/shard_map/ppermute | solution.py:419
  25.1 6.9 %collective-permute-start.3 = (bf16[160,128]{1,0:T(8,128)(2,1)S(1)}, bf16[160,128]{1,0:T(8,128)(2,1)S(1)}, u32[]{:S(2)}, u32[]{:S(2)}) collective-permute-start(bf16[160,128]{1,0:T(8,128)(2,1)S(1)} %collective-permute-done.2.far), channel_id=1, source_target_pairs={{0,64},{1,65},{2,66},{3,67},{4,68},{5,69},{6,70},{7,71},{8,72},{9,... | collective-permute-start | bytes 122888 | tf_op jit(solution)/shard_map/ppermute | solution.py:423
  26.4 5.6 %collective-permute-start.4 = (bf16[160,128]{1,0:T(8,128)(2,1)S(1)}, bf16[160,128]{1,0:T(8,128)(2,1)S(1)}, u32[]{:S(2)}, u32[]{:S(2)}) collective-permute-start(bf16[160,128]{1,0:T(8,128)(2,1)S(1)} %collective-permute-done.2.far), channel_id=1, source_target_pairs={{32,64},{33,65},{34,66},{35,67},{36,68},{37,69},{38,70},{39,71},{4... | collective-permute-start | bytes 122888 | tf_op jit(solution)/shard_map/ppermute | solution.py:422
  29.9 3.1 %collective-permute-start.5 = (bf16[160,128]{1,0:T(8,128)(2,1)S(1)}, bf16[160,128]{1,0:T(8,128)(2,1)S(1)}, u32[]{:S(2)}, u32[]{:S(2)}) collective-permute-start(bf16[160,128]{1,0:T(8,128)(2,1)S(1)} %collective-permute-done.2.far), channel_id=1, source_target_pairs={{0,32},{1,33},{2,34},{3,35},{4,36},{5,37},{6,38},{7,39},{8,40},{9,... | collective-permute-start | bytes 122888 | tf_op jit(solution)/shard_map/ppermute | solution.py:421

commit v5 on v4

--- a/solution.py
+++ b/solution.py
@@ -249,18 +249,20 @@
         dots[head] = dot_nt(jnp.where(own_lanes, d_attn[...], 0.0).astype(BF16), values[...])
 
     key_inv = [key_inverse[head : head + 1, :] for head in range(2)]
-    key_reach = [key_inv[head] * scales[head : head + 1, :] for head in range(2)]
-    scale_lanes = jnp.where(first, scales[0:1, :MODEL], scales[1:2, :MODEL])
+    wide = jnp.concatenate([scales[...]] * (KEYS // MODEL), axis=1)
+    key_reach = [key_inv[head] * wide[head : head + 1, :] for head in range(2)]
+    scale_lanes = jnp.where(first, scales[0:1, :], scales[1:2, :])
     scale_sums = [jnp.zeros((BLOCK, 1), F32), jnp.zeros((BLOCK, 1), F32)]
     for start in range(0, QUERIES, BLOCK):
         rows = slice(start, start + BLOCK)
+        width = NEAR if start < OWN else KEYS
         query_wide = queries[rows, :].astype(F32)
         norms = head_sums(query_wide * query_wide)
         for head in range(2):
             inverse = lax.rsqrt(norms[head] + EPSILON)
-            score = raw[head, rows, :] * (inverse * LOG2E) * key_reach[head] + bias[rows, :]
-            expo = jnp.exp2(score)
-            gain = dots[head, rows, :]
+            score = raw[head, rows, :width] * (inverse * LOG2E) * key_reach[head][:, :width]
+            expo = jnp.exp2(score + bias[rows, :width])
+            gain = dots[head, rows, :width]
             share = 1.0 / (jnp.sum(expo, axis=1, keepdims=True) + 1e-30)
             center = jnp.sum(expo * gain, axis=1, keepdims=True) * share
             if start < OWN:
@@ -355,7 +357,7 @@
         device(x + FIRST_X, y + FIRST_Y, z, core)
         for x in range(4)
         for y in range(4)
-        for core in range(2)
+        for core in (1, 0)
     ]
     for z in range(16)
 ]
@@ -400,7 +402,7 @@
     key_spots = np.zeros((2, 16, KEYS), np.float32)
     key_spots[:, :2] = TABLES
     key_spots = jnp.asarray(key_spots)
-    scales = jnp.broadcast_to(cos_scale[None, :, None], (4, 2, KEYS)).reshape(8, KEYS)
+    scales = jnp.broadcast_to(cos_scale[None, :, None], (4, 2, MODEL)).reshape(8, MODEL)
     tile_copy, weights, bias = pl.pallas_call(
         prepare_kernel,
         out_shape=(

time: 81 us -> 80.3 us (level)
  no operation moved by 1% of the time
where the time goes in v5:
time: 80.3 us; the launch traced here: 79.9 us
  blocking collectives  43.4 us (54%)
  starting transfers between devices  28.8 us (36%)
  Pallas kernels  3.23 us (4%)
  waiting for transfers between devices  1.95 us (2%)
  other arithmetic  1.38 us (2%)
  between operations  0.84 us (1%)
    all_to_all x3, blocking collectives, exchange(): lax.all_to_all(array, EVERY, 0, 0, axis_index_groups=groups, tiled=True)  43.4 us
    ppermute x1, starting transfers between devices, on_device(): next_chip = lax.ppermute(tile_copy, EVERY, NEXT_CHIP)  11.9 us
    ppermute x1, starting transfers between devices, on_device(): mate = lax.ppermute(mate_message, EVERY, CHIP_MATE)  8.79 us
    ppermute x1, starting transfers between devices, on_device(): far_next = lax.ppermute(far, EVERY, NEXT_CHIP)  3.56 us
    ppermute x1, starting transfers between devices, on_device(): far_mate = lax.ppermute(far, EVERY, CHIP_MATE)  1.92 us
    pallas_call x1, Pallas kernels, on_device(): pl.pallas_call(attention_kernel, out_shape=(jax.ShapeDtypeStruct((OWN, MO...  1.85 us
  transfers between devices with their start and end apart: 6, of which 2 were waited for; matrix products, arithmetic and copies ran while one was open for 0% of the time, Pallas kernels for 1%

profile of v5, /device:TPU:1, one launch (start us, length us, event | category | flops | bytes accessed | tf_op | source)
XLA Modules:
  0.0 79.9 jit_solution(2090050993219163184)
XLA Ops:
  0.6 0.0 copy-start.2
  0.6 0.8 pad_maximum_fusion.1.tile
  1.4 0.2 edges.1
  1.6 8.8 %collective-permute-start = (bf16[224,128]{1,0:T(8,128)(2,1)S(1)}, bf16[224,128]{1,0:T(8,128)(2,1)S(1)}, u32[]{:S(2)}, u32[]{:S(2)}) collective-permute-start(bf16[224,128]{1,0:T(8,128)(2,1)S(1)} %get-tuple-element.20), channel_id=1, source_target_pairs={{0,32},{1,33},{2,34},{3,35},{4,36},{5,37},{6,38},{7,39},{8,40},{9,... | collective-permute-start | bytes 172040 | tf_op jit(solution)/shard_map/ppermute | solution.py:399
  10.4 0.9 %collective-permute-done._.mate = bf16[224,128]{1,0:T(8,128)(2,1)S(1)} collective-permute-done((bf16[224,128]{1,0:T(8,128)(2,1)S(1)}, bf16[224,128]{1,0:T(8,128)(2,1)S(1)}, u32[]{:S(2)}, u32[]{:S(2)}) %collective-permute-start) | collective-permute-done | bytes 57376 | tf_op jit(solution)/shard_map/ppermute | solution.py:399
  11.3 1.3 %collective-permute-start.2 = (bf16[160,128]{1,0:T(8,128)(2,1)S(1)}, bf16[160,128]{1,0:T(8,128)(2,1)S(1)}, u32[]{:S(2)}, u32[]{:S(2)}) collective-permute-start(bf16[160,128]{1,0:T(8,128)(2,1)S(1)} %pad_maximum_fusion.2), channel_id=1, source_target_pairs={{0,1},{1,2},{2,3},{3,4},{4,5},{5,6},{6,7},{7,8},{8,9},{9,10},{10,1... | collective-permute-start | bytes 122888 | tf_op jit(solution)/shard_map/ppermute | solution.py:401
  12.6 0.0 copy-done.2
  12.6 0.0 copy-done
  12.6 0.0 copy-done.1
  12.6 0.5 prepare.1
  13.1 0.0 copy-start.3
  13.1 11.9 %collective-permute-start.1 = (bf16[256,128]{1,0:T(8,128)(2,1)S(1)}, bf16[256,128]{1,0:T(8,128)(2,1)S(1)}, u32[]{:S(2)}, u32[]{:S(2)}) collective-permute-start(bf16[256,128]{1,0:T(8,128)(2,1)S(1)} %get-tuple-element.22), channel_id=1, source_target_pairs={{32,64},{33,65},{34,66},{35,67},{36,68},{37,69},{38,70},{39,71},{4... | collective-permute-start | bytes 196616 | tf_op jit(solution)/shard_map/ppermute | solution.py:421
  25.1 0.0 collective-permute-done.2.far
  25.1 1.3 %collective-permute-start.3 = (bf16[160,128]{1,0:T(8,128)(2,1)S(1)}, bf16[160,128]{1,0:T(8,128)(2,1)S(1)}, u32[]{:S(2)}, u32[]{:S(2)}) collective-permute-start(bf16[160,128]{1,0:T(8,128)(2,1)S(1)} %collective-permute-done.2.far), channel_id=1, source_target_pairs={{0,64},{1,65},{2,66},{3,67},{4,68},{5,69},{6,70},{7,71},{8,72},{9,... | collective-permute-start | bytes 122888 | tf_op jit(solution)/shard_map/ppermute | solution.py:425
  26.4 3.6 %collective-permute-start.4 = (bf16[160,128]{1,0:T(8,128)(2,1)S(1)}, bf16[160,128]{1,0:T(8,128)(2,1)S(1)}, u32[]{:S(2)}, u32[]{:S(2)}) collective-permute-start(bf16[160,128]{1,0:T(8,128)(2,1)S(1)} %collective-permute-done.2.far), channel_id=1, source_target_pairs={{32,64},{33,65},{34,66},{35,67},{36,68},{37,69},{38,70},{39,71},{4... | collective-permute-start | bytes 122888 | tf_op jit(solution)/shard_map/ppermute | solution.py:424
  29.9 1.9 %collective-permute-start.5 = (bf16[160,128]{1,0:T(8,128)(2,1)S(1)}, bf16[160,128]{1,0:T(8,128)(2,1)S(1)}, u32[]{:S(2)}, u32[]{:S(2)}) collective-permute-start(bf16[160,128]{1,0:T(8,128)(2,1)S(1)} %collective-permute-done.2.far), channel_id=1, source_target_pairs={{0,32},{1,33},{2,34},{3,35},{4,36},{5,37},{6,38},{7,39},{8,40},{9,... | collective-permute-start | bytes 122888 | tf_op jit(solution)/shard_map/ppermute | solution.py:423
  31.9 0.0 copy-done.3
  31.9 0.1 broadcast_in_dim.60
  32.0 0.0 collective-permute-done.1.next_chip
  32.0 0.0 collective-permute-done.3.far_skip
  32.0 0.0 collective-permute-done.4.far_next
  32.0 1.1 %collective-permute-done.5.far_mate = bf16[160,128]{1,0:T(8,128)(2,1)S(1)} collective-permute-done((bf16[160,128]{1,0:T(8,128)(2,1)S(1)}, bf16[160,128]{1,0:T(8,128)(2,1)S(1)}, u32[]{:S(2)}, u32[]{:S(2)}) %collective-permute-start.5) | collective-permute-done | bytes 40992 | tf_op jit(solution)/shard_map/ppermute | solution.py:423
  33.0 0.1 broadcast_in_dim.61.scales
  33.1 1.8 %window_attention.1 = (bf16[128,128]{1,0:T(8,128)(2,1)S(1)}, bf16[512,128]{1,0:T(8,128)(2,1)S(1)}, bf16[8,128]{1,0:T(8,128)(2,1)S(1)}) custom-call(f32[8,128]{1,0:T(8,128)S(1)} %broadcast_in_dim.61.scales, bf16[256,128]{1,0:T(8,128)(2,1)S(1)} %pad_maximum_fusion.1.tile, bf16[512,128]{1,0:T(8,128)(2,1)S(1)} %get-tuple-element.21.weights, ...), custom_call_target="tpu_custom_call" | custom-call | tf_op jit(solution)/shard_map/window_attention/pallas_call | solution.py:426
  35.0 0.2 pad_maximum_fusion
  35.2 13.5 %all_to_all.15 = bf16[32,9,2,128]{3,2,1,0:T(2,128)(2,1)S(1)} all-to-all(bf16[32,9,2,128]{3,2,1,0:T(2,128)(2,1)S(1)} %pad_maximum_fusion), channel_id=1, replica_groups={{52,20,54,22,48,16,50,18,60,28,62,30,56,24,58,26,36,4,38,6,32,0,34,2,44..., dimensions={0} | all-to-all | bytes 294912 | tf_op jit(solution)/shard_map/all_to_all | solution.py:377
  48.7 0.1 convert_reduce_fusion
  48.9 0.1 fusion.3
  49.0 0.1 fusion.4
  49.1 18.2 %all_to_all.16 = bf16[16,9,2,128]{3,2,1,0:T(2,128)(2,1)S(1)} all-to-all(bf16[16,9,2,128]{3,2,1,0:T(2,128)(2,1)S(1)} %broadcast_in_dim.67), channel_id=1, replica_groups={{65,129,193,257,321,385,449,0,64,128,192,256,320,384,448,1},{97,161,225..., dimensions={0} | all-to-all | bytes 147456 | tf_op jit(solution)/shard_map/all_to_all | solution.py:377
  67.4 11.7 %all_to_all.17 = bf16[32,16,128]{2,1,0:T(8,128)(2,1)S(1)} all-to-all(bf16[32,16,128]{2,1,0:T(8,128)(2,1)S(1)} %broadcast_in_dim.68), channel_id=1, replica_groups={{52,20,54,22,48,16,50,18,60,28,62,30,56,24,58,26,36,4,38,6,32,0,34,2,44..., dimensions={0} | all-to-all | bytes 262144 | tf_op jit(solution)/shard_map/all_to_all | solution.py:377
  79.2 0.7 results.1
  (16 shorter events, 0.2 us)
Async XLA Ops:
  0.6 11.9 %copy-start.2 = (bf16[128,128]{1,0:T(8,128)(2,1)S(1)}, bf16[128,128]{1,0:T(8,128)(2,1)}, u32[]{:S(2)}) copy-start(bf16[128,128]{1,0:T(8,128)(2,1)} %w_out.1) | copy-start | bytes 98308
  1.4 11.2 %copy-start = (bf16[128,384]{1,0:T(8,128)(2,1)S(1)}, bf16[128,384]{1,0:T(8,128)(2,1)}, u32[]{:S(2)}) copy-start(bf16[128,384]{1,0:T(8,128)(2,1)} %w_qkv.1) | copy-start | bytes 294916
  1.4 11.2 %copy-start.1 = (f32[2,16,640]{2,1,0:T(8,128)S(1)}, f32[2,16,640]{2,1,0:T(8,128)}, u32[]{:S(2)}) copy-start(f32[2,16,640]{2,1,0:T(8,128)} %constant.10.clone.key_spots) | copy-start | bytes 245764
  1.6 9.7 %collective-permute-start = (bf16[224,128]{1,0:T(8,128)(2,1)S(1)}, bf16[224,128]{1,0:T(8,128)(2,1)S(1)}, u32[]{:S(2)}, u32[]{:S(2)}) collective-permute-start(bf16[224,128]{1,0:T(8,128)(2,1)S(1)} %get-tuple-element.20), channel_id=1, source_target_pairs={{0,32},{1,33},{2,34},{3,35},{4,36},{5,37},{6,38},{7,39},{8,40},{9,... | collective-permute-start | bytes 172040 | tf_op jit(solution)/shard_map/ppermute | solution.py:399
  11.3 13.8 %collective-permute-start.2 = (bf16[160,128]{1,0:T(8,128)(2,1)S(1)}, bf16[160,128]{1,0:T(8,128)(2,1)S(1)}, u32[]{:S(2)}, u32[]{:S(2)}) collective-permute-start(bf16[160,128]{1,0:T(8,128)(2,1)S(1)} %pad_maximum_fusion.2), channel_id=1, source_target_pairs={{0,1},{1,2},{2,3},{3,4},{4,5},{5,6},{6,7},{7,8},{8,9},{9,10},{10,1... | collective-permute-start | bytes 122888 | tf_op jit(solution)/shard_map/ppermute | solution.py:401
  13.1 18.8 %copy-start.3 = (f32[2]{0:T(128)S(1)}, f32[2]{0:T(128)}, u32[]{:S(2)}) copy-start(f32[2]{0:T(128)} %param.10) | copy-start | bytes 28
  13.1 18.9 %collective-permute-start.1 = (bf16[256,128]{1,0:T(8,128)(2,1)S(1)}, bf16[256,128]{1,0:T(8,128)(2,1)S(1)}, u32[]{:S(2)}, u32[]{:S(2)}) collective-permute-start(bf16[256,128]{1,0:T(8,128)(2,1)S(1)} %get-tuple-element.22), channel_id=1, source_target_pairs={{32,64},{33,65},{34,66},{35,67},{36,68},{37,69},{38,70},{39,71},{4... | collective-permute-start | bytes 196616 | tf_op jit(solution)/shard_map/ppermute | solution.py:421
  25.1 6.9 %collective-permute-start.3 = (bf16[160,128]{1,0:T(8,128)(2,1)S(1)}, bf16[160,128]{1,0:T(8,128)(2,1)S(1)}, u32[]{:S(2)}, u32[]{:S(2)}) collective-permute-start(bf16[160,128]{1,0:T(8,128)(2,1)S(1)} %collective-permute-done.2.far), channel_id=1, source_target_pairs={{0,64},{1,65},{2,66},{3,67},{4,68},{5,69},{6,70},{7,71},{8,72},{9,... | collective-permute-start | bytes 122888 | tf_op jit(solution)/shard_map/ppermute | solution.py:425
  26.4 5.6 %collective-permute-start.4 = (bf16[160,128]{1,0:T(8,128)(2,1)S(1)}, bf16[160,128]{1,0:T(8,128)(2,1)S(1)}, u32[]{:S(2)}, u32[]{:S(2)}) collective-permute-start(bf16[160,128]{1,0:T(8,128)(2,1)S(1)} %collective-permute-done.2.far), channel_id=1, source_target_pairs={{32,64},{33,65},{34,66},{35,67},{36,68},{37,69},{38,70},{39,71},{4... | collective-permute-start | bytes 122888 | tf_op jit(solution)/shard_map/ppermute | solution.py:424
  29.9 3.1 %collective-permute-start.5 = (bf16[160,128]{1,0:T(8,128)(2,1)S(1)}, bf16[160,128]{1,0:T(8,128)(2,1)S(1)}, u32[]{:S(2)}, u32[]{:S(2)}) collective-permute-start(bf16[160,128]{1,0:T(8,128)(2,1)S(1)} %collective-permute-done.2.far), channel_id=1, source_target_pairs={{0,32},{1,33},{2,34},{3,35},{4,36},{5,37},{6,38},{7,39},{8,40},{9,... | collective-permute-start | bytes 122888 | tf_op jit(solution)/shard_map/ppermute | solution.py:423

commit v6 on v5

--- a/solution.py
+++ b/solution.py
@@ -352,14 +352,16 @@
 
 
 FIRST_X, FIRST_Y, FIRST_Z = 2, 2, 9
+def apart(place):
+    return min(place[0], 4 - place[0]) + min(place[1], 4 - place[1])
+
+
+PLACES = sorted(
+    ((x, y, core) for x in range(4) for y in range(4) for core in (1, 0)),
+    key=lambda place: (place != (0, 0, 1), -apart(place)),
+)
 PLANES = [
-    [
-        device(x + FIRST_X, y + FIRST_Y, z, core)
-        for x in range(4)
-        for y in range(4)
-        for core in (1, 0)
-    ]
-    for z in range(16)
+    [device(x + FIRST_X, y + FIRST_Y, z, core) for x, y, core in PLACES] for z in range(16)
 ]
 LINES = [
     [device(x, y, z + FIRST_Z, core) for z in range(16)]

time: 80.3 us -> 79.9 us (level)
  no operation moved by 1% of the time
where the time goes in v6:
time: 79.9 us; the launch traced here: 79.5 us
  blocking collectives  43 us (54%)
  starting transfers between devices  28.8 us (36%)
  Pallas kernels  3.23 us (4%)
  waiting for transfers between devices  1.95 us (2%)
  other arithmetic  1.38 us (2%)
  between operations  0.84 us (1%)
    all_to_all x3, blocking collectives, exchange(): lax.all_to_all(array, EVERY, 0, 0, axis_index_groups=groups, tiled=True)  43 us
    ppermute x1, starting transfers between devices, on_device(): next_chip = lax.ppermute(tile_copy, EVERY, NEXT_CHIP)  11.9 us
    ppermute x1, starting transfers between devices, on_device(): mate = lax.ppermute(mate_message, EVERY, CHIP_MATE)  8.79 us
    ppermute x1, starting transfers between devices, on_device(): far_next = lax.ppermute(far, EVERY, NEXT_CHIP)  3.56 us
    ppermute x1, starting transfers between devices, on_device(): far_mate = lax.ppermute(far, EVERY, CHIP_MATE)  1.92 us
    pallas_call x1, Pallas kernels, on_device(): pl.pallas_call(attention_kernel, out_shape=(jax.ShapeDtypeStruct((OWN, MO...  1.85 us
  transfers between devices with their start and end apart: 6, of which 2 were waited for; matrix products, arithmetic and copies ran while one was open for 0% of the time, Pallas kernels for 1%

profile of v6, /device:TPU:1, one launch (start us, length us, event | category | flops | bytes accessed | tf_op | source)
XLA Modules:
  0.0 79.5 jit_solution(5773348239214865363)
XLA Ops:
  0.6 0.0 copy-start.2
  0.6 0.8 pad_maximum_fusion.1.tile
  1.4 0.2 edges.1
  1.6 8.8 %collective-permute-start = (bf16[224,128]{1,0:T(8,128)(2,1)S(1)}, bf16[224,128]{1,0:T(8,128)(2,1)S(1)}, u32[]{:S(2)}, u32[]{:S(2)}) collective-permute-start(bf16[224,128]{1,0:T(8,128)(2,1)S(1)} %get-tuple-element.20), channel_id=1, source_target_pairs={{0,32},{1,33},{2,34},{3,35},{4,36},{5,37},{6,38},{7,39},{8,40},{9,... | collective-permute-start | bytes 172040 | tf_op jit(solution)/shard_map/ppermute | solution.py:401
  10.4 0.9 %collective-permute-done._.mate = bf16[224,128]{1,0:T(8,128)(2,1)S(1)} collective-permute-done((bf16[224,128]{1,0:T(8,128)(2,1)S(1)}, bf16[224,128]{1,0:T(8,128)(2,1)S(1)}, u32[]{:S(2)}, u32[]{:S(2)}) %collective-permute-start) | collective-permute-done | bytes 57376 | tf_op jit(solution)/shard_map/ppermute | solution.py:401
  11.3 1.3 %collective-permute-start.2 = (bf16[160,128]{1,0:T(8,128)(2,1)S(1)}, bf16[160,128]{1,0:T(8,128)(2,1)S(1)}, u32[]{:S(2)}, u32[]{:S(2)}) collective-permute-start(bf16[160,128]{1,0:T(8,128)(2,1)S(1)} %pad_maximum_fusion.2), channel_id=1, source_target_pairs={{0,1},{1,2},{2,3},{3,4},{4,5},{5,6},{6,7},{7,8},{8,9},{9,10},{10,1... | collective-permute-start | bytes 122888 | tf_op jit(solution)/shard_map/ppermute | solution.py:403
  12.6 0.0 copy-done.2
  12.6 0.0 copy-done
  12.6 0.0 copy-done.1
  12.6 0.5 prepare.1
  13.1 0.0 copy-start.3
  13.1 11.9 %collective-permute-start.1 = (bf16[256,128]{1,0:T(8,128)(2,1)S(1)}, bf16[256,128]{1,0:T(8,128)(2,1)S(1)}, u32[]{:S(2)}, u32[]{:S(2)}) collective-permute-start(bf16[256,128]{1,0:T(8,128)(2,1)S(1)} %get-tuple-element.22), channel_id=1, source_target_pairs={{32,64},{33,65},{34,66},{35,67},{36,68},{37,69},{38,70},{39,71},{4... | collective-permute-start | bytes 196616 | tf_op jit(solution)/shard_map/ppermute | solution.py:423
  25.1 0.0 collective-permute-done.2.far
  25.1 1.3 %collective-permute-start.3 = (bf16[160,128]{1,0:T(8,128)(2,1)S(1)}, bf16[160,128]{1,0:T(8,128)(2,1)S(1)}, u32[]{:S(2)}, u32[]{:S(2)}) collective-permute-start(bf16[160,128]{1,0:T(8,128)(2,1)S(1)} %collective-permute-done.2.far), channel_id=1, source_target_pairs={{0,64},{1,65},{2,66},{3,67},{4,68},{5,69},{6,70},{7,71},{8,72},{9,... | collective-permute-start | bytes 122888 | tf_op jit(solution)/shard_map/ppermute | solution.py:427
  26.4 3.6 %collective-permute-start.4 = (bf16[160,128]{1,0:T(8,128)(2,1)S(1)}, bf16[160,128]{1,0:T(8,128)(2,1)S(1)}, u32[]{:S(2)}, u32[]{:S(2)}) collective-permute-start(bf16[160,128]{1,0:T(8,128)(2,1)S(1)} %collective-permute-done.2.far), channel_id=1, source_target_pairs={{32,64},{33,65},{34,66},{35,67},{36,68},{37,69},{38,70},{39,71},{4... | collective-permute-start | bytes 122888 | tf_op jit(solution)/shard_map/ppermute | solution.py:426
  29.9 1.9 %collective-permute-start.5 = (bf16[160,128]{1,0:T(8,128)(2,1)S(1)}, bf16[160,128]{1,0:T(8,128)(2,1)S(1)}, u32[]{:S(2)}, u32[]{:S(2)}) collective-permute-start(bf16[160,128]{1,0:T(8,128)(2,1)S(1)} %collective-permute-done.2.far), channel_id=1, source_target_pairs={{0,32},{1,33},{2,34},{3,35},{4,36},{5,37},{6,38},{7,39},{8,40},{9,... | collective-permute-start | bytes 122888 | tf_op jit(solution)/shard_map/ppermute | solution.py:425
  31.9 0.0 copy-done.3
  31.9 0.1 broadcast_in_dim.60
  32.0 0.0 collective-permute-done.1.next_chip
  32.0 0.0 collective-permute-done.3.far_skip
  32.0 0.0 collective-permute-done.4.far_next
  32.0 1.1 %collective-permute-done.5.far_mate = bf16[160,128]{1,0:T(8,128)(2,1)S(1)} collective-permute-done((bf16[160,128]{1,0:T(8,128)(2,1)S(1)}, bf16[160,128]{1,0:T(8,128)(2,1)S(1)}, u32[]{:S(2)}, u32[]{:S(2)}) %collective-permute-start.5) | collective-permute-done | bytes 40992 | tf_op jit(solution)/shard_map/ppermute | solution.py:425
  33.0 0.1 broadcast_in_dim.61.scales
  33.1 1.8 %window_attention.1 = (bf16[128,128]{1,0:T(8,128)(2,1)S(1)}, bf16[512,128]{1,0:T(8,128)(2,1)S(1)}, bf16[8,128]{1,0:T(8,128)(2,1)S(1)}) custom-call(f32[8,128]{1,0:T(8,128)S(1)} %broadcast_in_dim.61.scales, bf16[256,128]{1,0:T(8,128)(2,1)S(1)} %pad_maximum_fusion.1.tile, bf16[512,128]{1,0:T(8,128)(2,1)S(1)} %get-tuple-element.21.weights, ...), custom_call_target="tpu_custom_call" | custom-call | tf_op jit(solution)/shard_map/window_attention/pallas_call | solution.py:428
  35.0 0.2 pad_maximum_fusion
  35.2 13.5 %all_to_all.15 = bf16[32,9,2,128]{3,2,1,0:T(2,128)(2,1)S(1)} all-to-all(bf16[32,9,2,128]{3,2,1,0:T(2,128)(2,1)S(1)} %pad_maximum_fusion), channel_id=1, replica_groups={{52,32,0,56,24,38,6,34,2,40,8,48,16,62,30,58,26,36,4,46,14,42,10,54,22,..., dimensions={0} | all-to-all | bytes 294912 | tf_op jit(solution)/shard_map/all_to_all | solution.py:379
  48.7 0.1 convert_reduce_fusion
  48.9 0.1 fusion.3
  49.0 0.1 fusion.4
  49.2 18.4 %all_to_all.16 = bf16[16,9,2,128]{3,2,1,0:T(2,128)(2,1)S(1)} all-to-all(bf16[16,9,2,128]{3,2,1,0:T(2,128)(2,1)S(1)} %broadcast_in_dim.67), channel_id=1, replica_groups={{65,129,193,257,321,385,449,0,64,128,192,256,320,384,448,1},{97,161,225..., dimensions={0} | all-to-all | bytes 147456 | tf_op jit(solution)/shard_map/all_to_all | solution.py:379
  67.7 11.1 %all_to_all.17 = bf16[32,16,128]{2,1,0:T(8,128)(2,1)S(1)} all-to-all(bf16[32,16,128]{2,1,0:T(8,128)(2,1)S(1)} %broadcast_in_dim.68), channel_id=1, replica_groups={{52,32,0,56,24,38,6,34,2,40,8,48,16,62,30,58,26,36,4,46,14,42,10,54,22,..., dimensions={0} | all-to-all | bytes 262144 | tf_op jit(solution)/shard_map/all_to_all | solution.py:379
  78.8 0.7 results.1
  (16 shorter events, 0.2 us)
Async XLA Ops:
  0.6 11.9 %copy-start.2 = (bf16[128,128]{1,0:T(8,128)(2,1)S(1)}, bf16[128,128]{1,0:T(8,128)(2,1)}, u32[]{:S(2)}) copy-start(bf16[128,128]{1,0:T(8,128)(2,1)} %w_out.1) | copy-start | bytes 98308
  1.4 11.2 %copy-start = (bf16[128,384]{1,0:T(8,128)(2,1)S(1)}, bf16[128,384]{1,0:T(8,128)(2,1)}, u32[]{:S(2)}) copy-start(bf16[128,384]{1,0:T(8,128)(2,1)} %w_qkv.1) | copy-start | bytes 294916
  1.4 11.2 %copy-start.1 = (f32[2,16,640]{2,1,0:T(8,128)S(1)}, f32[2,16,640]{2,1,0:T(8,128)}, u32[]{:S(2)}) copy-start(f32[2,16,640]{2,1,0:T(8,128)} %constant.10.clone.key_spots) | copy-start | bytes 245764
  1.6 9.7 %collective-permute-start = (bf16[224,128]{1,0:T(8,128)(2,1)S(1)}, bf16[224,128]{1,0:T(8,128)(2,1)S(1)}, u32[]{:S(2)}, u32[]{:S(2)}) collective-permute-start(bf16[224,128]{1,0:T(8,128)(2,1)S(1)} %get-tuple-element.20), channel_id=1, source_target_pairs={{0,32},{1,33},{2,34},{3,35},{4,36},{5,37},{6,38},{7,39},{8,40},{9,... | collective-permute-start | bytes 172040 | tf_op jit(solution)/shard_map/ppermute | solution.py:401
  11.3 13.8 %collective-permute-start.2 = (bf16[160,128]{1,0:T(8,128)(2,1)S(1)}, bf16[160,128]{1,0:T(8,128)(2,1)S(1)}, u32[]{:S(2)}, u32[]{:S(2)}) collective-permute-start(bf16[160,128]{1,0:T(8,128)(2,1)S(1)} %pad_maximum_fusion.2), channel_id=1, source_target_pairs={{0,1},{1,2},{2,3},{3,4},{4,5},{5,6},{6,7},{7,8},{8,9},{9,10},{10,1... | collective-permute-start | bytes 122888 | tf_op jit(solution)/shard_map/ppermute | solution.py:403
  13.1 18.8 %copy-start.3 = (f32[2]{0:T(128)S(1)}, f32[2]{0:T(128)}, u32[]{:S(2)}) copy-start(f32[2]{0:T(128)} %param.10) | copy-start | bytes 28
  13.1 18.9 %collective-permute-start.1 = (bf16[256,128]{1,0:T(8,128)(2,1)S(1)}, bf16[256,128]{1,0:T(8,128)(2,1)S(1)}, u32[]{:S(2)}, u32[]{:S(2)}) collective-permute-start(bf16[256,128]{1,0:T(8,128)(2,1)S(1)} %get-tuple-element.22), channel_id=1, source_target_pairs={{32,64},{33,65},{34,66},{35,67},{36,68},{37,69},{38,70},{39,71},{4... | collective-permute-start | bytes 196616 | tf_op jit(solution)/shard_map/ppermute | solution.py:423
  25.1 6.9 %collective-permute-start.3 = (bf16[160,128]{1,0:T(8,128)(2,1)S(1)}, bf16[160,128]{1,0:T(8,128)(2,1)S(1)}, u32[]{:S(2)}, u32[]{:S(2)}) collective-permute-start(bf16[160,128]{1,0:T(8,128)(2,1)S(1)} %collective-permute-done.2.far), channel_id=1, source_target_pairs={{0,64},{1,65},{2,66},{3,67},{4,68},{5,69},{6,70},{7,71},{8,72},{9,... | collective-permute-start | bytes 122888 | tf_op jit(solution)/shard_map/ppermute | solution.py:427
  26.4 5.6 %collective-permute-start.4 = (bf16[160,128]{1,0:T(8,128)(2,1)S(1)}, bf16[160,128]{1,0:T(8,128)(2,1)S(1)}, u32[]{:S(2)}, u32[]{:S(2)}) collective-permute-start(bf16[160,128]{1,0:T(8,128)(2,1)S(1)} %collective-permute-done.2.far), channel_id=1, source_target_pairs={{32,64},{33,65},{34,66},{35,67},{36,68},{37,69},{38,70},{39,71},{4... | collective-permute-start | bytes 122888 | tf_op jit(solution)/shard_map/ppermute | solution.py:426
  29.9 3.1 %collective-permute-start.5 = (bf16[160,128]{1,0:T(8,128)(2,1)S(1)}, bf16[160,128]{1,0:T(8,128)(2,1)S(1)}, u32[]{:S(2)}, u32[]{:S(2)}) collective-permute-start(bf16[160,128]{1,0:T(8,128)(2,1)S(1)} %collective-permute-done.2.far), channel_id=1, source_target_pairs={{0,32},{1,33},{2,34},{3,35},{4,36},{5,37},{6,38},{7,39},{8,40},{9,... | collective-permute-start | bytes 122888 | tf_op jit(solution)/shard_map/ppermute | solution.py:425
